TPU v7x, 512 devices: a whole 4x4x16 slice. The times are simulated.
512 devices in a mesh: gx: 16 (over x, y), gy: 4 (over z_hi), gz: 8 (over z_lo, core).
Axes of the slice: x: 4, y: 4, z: 16 (z_hi: 4, z_lo: 4; z = z_hi * 4 + z_lo), core: 2. Of those that a mesh axis runs over, the one named last changes fastest.
Arguments:
- scalars: float32 [20, 524288], P(None, ('gx', 'gy', 'gz')), may hold values from -6 to 6
- particle_mass: float32 [524288], P(('gx', 'gy', 'gz')), may hold values from 0.5 to 2
- cell_first: int32 [524288], P(('gx', 'gy', 'gz')), may hold values from 0 to 511
- cell_second: int32 [524288], P(('gx', 'gy', 'gz')), may hold values from 0 to 511
- cell_final: int32 [524288], P(('gx', 'gy', 'gz')), may hold values from 0 to 511
- offset_first: float32 [3, 524288], P(None, ('gx', 'gy', 'gz')), may hold values from -0.5 to 0.5
- offset_second: float32 [3, 524288], P(None, ('gx', 'gy', 'gz')), may hold values from -0.5 to 0.5
- face_first: int32 [524288], P(('gx', 'gy', 'gz')), may hold values from 0 to 6, as said below
- face_second: int32 [524288], P(('gx', 'gy', 'gz')), may hold values from 0 to 6, as said below
- mean_field: float32 [20, 128, 32, 64], P(None, 'gx', 'gy', 'gz'), may hold values from -6 to 6
- mix_rate: float32 [128, 32, 64], P('gx', 'gy', 'gz'), may hold values from 0.25 to 2
- react_in: float32 [128, 20], replicated, may hold values from -1.25 to 1.25
- hidden_bias: float32 [128], replicated, may hold values from -4 to 4
- react_out: float32 [20, 128], replicated, may hold values from -0.5 to 0.5
Outputs:
- cell_mean: float32 [20, 128, 32, 64], P(None, 'gx', 'gy', 'gz')
Inputs may be any that keep to these rules, and one draw needn't show every extreme that they name: `face_first`: on one owner at most 64 particles carry the same nonzero code, and some owner has exactly 64 with one code. A particle with a nonzero face_first has face_second 0; on one owner at most 64 particles carry the same nonzero code, and some owner has exactly 64 with one code.
All inputs are finite; a program needn't handle non-finite values.
Results may differ from a plain program's by a relative error of at most 0.00005.
Values sent between devices are 32-bit elements; how exact they have to be, the bound alone decides.
A program may use at most 64 MiB of HBM per device.

v0:
```python
import jax
import jax.numpy as jnp
from jax import lax
from jax.sharding import PartitionSpec as P

IEM_FACTOR = 0.4
TIME_STEP = 0.4
PRIOR_MASS = 2.0


def extended_2(block, sides, width, periodic):
    for axis, dim in sides:
        count = lax.axis_size(axis)
        forward = [(i, i + 1) for i in range(count - 1)]
        if periodic:
            forward.append((count - 1, 0))
        backward = [(target, source) for source, target in forward]
        low = lax.ppermute(
            lax.slice_in_dim(block, block.shape[dim] - width, None, axis=dim), axis, forward
        )
        high = lax.ppermute(lax.slice_in_dim(block, 0, width, axis=dim), axis, backward)
        block = jnp.concatenate([low, block, high], axis=dim)
    return block


def shifted(block, axis, distance):
    devices = range(lax.axis_size(axis))
    route = [(i - distance, i) for i in devices if i - distance in devices]
    return lax.ppermute(block, axis, route)


def from_behind(x, axis, by):
    size = lax.axis_size(axis)
    return lax.ppermute(x, axis, [(i, (i + by) % size) for i in range(size)])


def spline(position):
    return (0.5 * (0.5 - position) ** 2, 0.75 - position * position, 0.5 * (0.5 + position) ** 2)


def interpolate(flat_field, base_index, strides, offsets):
    along_x = spline(offsets[0])
    along_y = spline(offsets[1])
    along_z = spline(offsets[2])
    terms = []
    for step_a in range(3):
        for step_b in range(3):
            for step_e in range(3):
                flat_shift = (step_a - 1) * strides[0] + (step_b - 1) * strides[1] + (step_e - 1)
                weight = along_x[step_a] * along_y[step_b] * along_z[step_e]
                terms.append(
                    weight[None, :] * jnp.take(flat_field, base_index + flat_shift, axis=1)
                )
    return sum(terms[1:], terms[0])


def mixing(values, sampled):
    count_s = values.shape[0]
    return values - IEM_FACTOR * sampled[count_s][None, :] * (values - sampled[:count_s])


def reaction(values, react_in, hidden_bias, react_out):
    hidden = jnp.tanh(
        jnp.dot(react_in, values, precision=lax.Precision.HIGHEST) + hidden_bias[:, None]
    )
    return values + TIME_STEP * jnp.dot(react_out, hidden, precision=lax.Precision.HIGHEST)


def cell_average(values, masses, cells, field_now):
    ncells = field_now.shape[1] * field_now.shape[2] * field_now.shape[3]
    weighted = jax.ops.segment_sum((values * masses[None, :]).T, cells, num_segments=ncells)
    weights_sum = jax.ops.segment_sum(masses, cells, num_segments=ncells)
    return (weighted.T.reshape(field_now.shape) + PRIOR_MASS * field_now) / (
        weights_sum.reshape(field_now.shape[1:])[None] + PRIOR_MASS
    )


def extend(field_now):
    azimuth_ext = extended_2(field_now, (("gz", 3),), 1, True)
    return extended_2(azimuth_ext, (("gx", 1), ("gy", 2)), 1, False)


def sample_local(extended, cells, offsets, field_shape):
    strides = (extended.shape[2] * extended.shape[3], extended.shape[3])
    cell_x = cells // (field_shape[2] * field_shape[3])
    cell_y = cells // field_shape[3] % field_shape[2]
    cell_z = cells % field_shape[3]
    base_index = (cell_x + 1) * strides[0] + (cell_y + 1) * strides[1] + cell_z + 1
    flat_field = extended.reshape(extended.shape[0], -1)
    return interpolate(flat_field, base_index, strides, offsets)


def pack(faces, floats, integers, capacity):
    sorted_rows = jnp.argsort(faces, stable=True)
    code_list = jnp.arange(7, dtype=jnp.int32)
    counts = jnp.sum((faces[None, :] == code_list[:, None]).astype(jnp.int32), axis=1)
    starts = jnp.cumsum(counts) - counts
    sorted_floats = jnp.concatenate(
        [
            jnp.take(floats, sorted_rows, axis=1),
            jnp.zeros((floats.shape[0], capacity), jnp.float32),
        ],
        axis=1,
    )
    sorted_ints = jnp.concatenate(
        [
            jnp.take(integers, sorted_rows, axis=1),
            jnp.zeros((integers.shape[0], capacity), jnp.int32),
        ],
        axis=1,
    )
    slot_rows = jnp.arange(capacity, dtype=jnp.int32)
    blocks = []
    for code in range(1, 7):
        live_rows = slot_rows < counts[code]
        float_block = jnp.where(
            live_rows[None, :],
            lax.dynamic_slice_in_dim(sorted_floats, starts[code], capacity, 1),
            0.0,
        )
        int_block = jnp.where(
            live_rows[None, :], lax.dynamic_slice_in_dim(sorted_ints, starts[code], capacity, 1), 0
        )
        blocks.append((float_block, int_block))
    return blocks


def migrate(faces, floats, integers, capacity):
    blocks = pack(faces, floats, integers, capacity)
    arrived = []
    for step_sign, block_id in ((1, 0), (-1, 1)):
        arrived.append(shifted((blocks[block_id][0], blocks[block_id][1]), "gx", step_sign))
    for step_sign, block_id in ((1, 2), (-1, 3)):
        arrived.append(shifted((blocks[block_id][0], blocks[block_id][1]), "gy", step_sign))
    for step_sign, block_id in ((1, 4), (-1, 5)):
        arrived.append(from_behind((blocks[block_id][0], blocks[block_id][1]), "gz", step_sign))
    floats_in = jnp.concatenate([entry[0] for entry in arrived], axis=1)
    ints_in = jnp.concatenate([entry[1] for entry in arrived], axis=1)
    return (floats_in, ints_in)


def shards(
    scalars,
    particle_mass,
    cell_first,
    cell_second,
    cell_final,
    offset_first,
    offset_second,
    face_first,
    face_second,
    mean_field,
    mix_rate,
    react_in,
    hidden_bias,
    react_out,
):
    count_s = scalars.shape[0]
    slots = scalars.shape[1]
    capacity = slots // 16
    field_shape = mean_field.shape
    extended_first = extend(jnp.concatenate([mean_field, mix_rate[None]], axis=0))
    mixed_first = mixing(
        scalars, sample_local(extended_first, cell_first, offset_first, field_shape)
    )
    stay_mass = particle_mass * (face_first == 0).astype(jnp.float32)
    carried_ints = jnp.stack([cell_second, cell_final])
    reacted_first = reaction(mixed_first, react_in, hidden_bias, react_out)
    floats_in, ints_in = migrate(
        face_first,
        jnp.concatenate([reacted_first, particle_mass[None], offset_second], axis=0),
        carried_ints,
        capacity,
    )
    arrived_first = floats_in[:count_s]
    values_all = jnp.concatenate([reacted_first, arrived_first], axis=1)
    masses_all = jnp.concatenate([stay_mass, floats_in[count_s]])
    offsets_all = jnp.concatenate([offset_second, floats_in[count_s + 1 :]], axis=1)
    cells_second = jnp.concatenate([cell_second, ints_in[0]])
    cells_final = jnp.concatenate([cell_final, ints_in[1]])
    field_second = cell_average(values_all, masses_all, cells_second, mean_field)
    extended_second = jnp.concatenate([extend(field_second), extended_first[count_s:]], axis=0)
    mixed_second = mixing(
        values_all, sample_local(extended_second, cells_second, offsets_all, field_shape)
    )
    mover_ints = cell_final[None]
    reacted_second = reaction(mixed_second, react_in, hidden_bias, react_out)
    floats_out, ints_out = migrate(
        face_second,
        jnp.concatenate([reacted_second[:, :slots], stay_mass[None]], axis=0),
        mover_ints,
        capacity,
    )
    arrived_second = floats_out[:count_s]
    kept_mass = jnp.concatenate(
        [
            stay_mass * (face_second == 0).astype(jnp.float32),
            masses_all[slots:],
            floats_out[count_s],
        ]
    )
    values_last = jnp.concatenate([reacted_second, arrived_second], axis=1)
    cells_last = jnp.concatenate([cells_final, ints_out[0]])
    return cell_average(values_last, kept_mass, cells_last, field_second)


def solution(mesh):
    in_specs = (
        P(None, ("gx", "gy", "gz")),
        P(("gx", "gy", "gz")),
        P(("gx", "gy", "gz")),
        P(("gx", "gy", "gz")),
        P(("gx", "gy", "gz")),
        P(None, ("gx", "gy", "gz")),
        P(None, ("gx", "gy", "gz")),
        P(("gx", "gy", "gz")),
        P(("gx", "gy", "gz")),
        P(None, "gx", "gy", "gz"),
        P("gx", "gy", "gz"),
        P(),
        P(),
        P(),
    )
    out_specs = P(None, "gx", "gy", "gz")
    return jax.shard_map(shards, mesh=mesh, in_specs=in_specs, out_specs=out_specs, check_vma=False)
```

profile of v0, /device:TPU:483, one launch (start us, length us, event | category | flops | bytes accessed | tf_op | source)
XLA Modules:
  0.0 523.7 jit_solution(10787557950430312249)
XLA Ops:
  9.8 4.4 sort.31
  16.2 4.4 sort.32
  32.3 3.2 collective-permute-start
  35.5 4.2 collective-permute-start.1
  41.0 7.9 %collective-permute-start.3 = (s32[2,64]{0,1:T(8,128)S(1)}, s32[2,64]{0,1:T(8,128)S(1)}, u32[]{:S(2)}, u32[]{:S(2)}) collective-permute-start(s32[2,64]{0,1:T(8,128)S(1)} %get-tuple-element.67), channel_id=1, source_target_pairs={{8,0},{16,8},{24,16},{9,1},{17,9},{25,17},{10,2},{18,10},{26,18},{... | collective-permute-start | bytes 1544 | tf_op jit(solution)/shard_map/ppermute | solution.py:29
  48.9 5.2 collective-permute-start.4
  64.1 4.5 gather_fusion.1
  86.3 5.2 collective-permute-start.12
  112.5 3.7 collective-permute-done.14
  116.4 5.2 collective-permute-start.17
  123.8 10.7 %collective-permute-done.16 = f32[21,10,1,10]{0,3,2,1:T(8,128)S(1)} collective-permute-done((f32[21,10,1,10]{0,3,2,1:T(8,128)S(1)}, f32[21,10,1,10]{0,3,2,1:T(8,128)S(1)}, u32[]{:S(2)}, u32[]{:S(2)}) %collective-permute-start.16) | collective-permute-done | bytes 8432 | tf_op jit(solution)/shard_map/ppermute | solution.py:18
  237.6 5.6 %collective-permute-start.19 = (f32[24,64]{1,0:T(8,128)S(1)}, f32[24,64]{1,0:T(8,128)S(1)}, u32[]{:S(2)}, u32[]{:S(2)}) collective-permute-start(f32[24,64]{1,0:T(8,128)S(1)} %get-tuple-element.83), channel_id=1, source_target_pairs={{32,0},{64,32},{96,64},{128,96},{160,128},{192,160},{224,192},{256... | collective-permute-start | bytes 18440 | tf_op jit(solution)/shard_map/ppermute | solution.py:29
  244.5 7.9 %collective-permute-start.21 = (f32[24,64]{1,0:T(8,128)S(1)}, f32[24,64]{1,0:T(8,128)S(1)}, u32[]{:S(2)}, u32[]{:S(2)}) collective-permute-start(f32[24,64]{1,0:T(8,128)S(1)} %get-tuple-element.85), channel_id=1, source_target_pairs={{8,0},{16,8},{24,16},{9,1},{17,9},{25,17},{10,2},{18,10},{26,18},{... | collective-permute-start | bytes 18440 | tf_op jit(solution)/shard_map/ppermute | solution.py:29
  252.4 5.8 %collective-permute-start.22 = (f32[24,64]{1,0:T(8,128)S(1)}, f32[24,64]{1,0:T(8,128)S(1)}, u32[]{:S(2)}, u32[]{:S(2)}) collective-permute-start(f32[24,64]{1,0:T(8,128)S(1)} %get-tuple-element.86), channel_id=1, source_target_pairs={{0,1},{1,2},{2,3},{3,4},{4,5},{5,6},{6,7},{7,0},{8,9},{9,10},{10,1... | collective-permute-start | bytes 18440 | tf_op jit(solution)/shard_map/ppermute | solution.py:34
  260.7 4.2 collective-permute-done.23
  266.0 21.5 %scatter_custom_fusion.1 = f32[512]{0:T(512)S(1)} fusion(s32[1408]{0:T(1024)} %pad_add_fusion.2, f32[1408]{0:T(1024)S(1)} %pad_maximum_fusion.25, f32[]{:T(128)} %constant.305.clone.1), kind=kCustom, calls=%fused_computation.550 | custom fusion | flops 1408 | bytes 2560 | tf_op jit(solution)/shard_map/scatter-add | solution.py:72
  287.6 9.5 %scatter_custom_fusion = f32[512,20]{1,0:T(8,128)S(1)} fusion(s32[1408]{0:T(1024)} %pad_add_fusion.2, f32[1408,20]{1,0:T(8,128)S(1)} %copy.243, f32[]{:T(128)} %constant.263.clone.1), kind=kCustom, calls=%fused_computation.145 | custom fusion | flops 28160 | bytes 41472 | tf_op jit(solution)/shard_map/scatter-add | solution.py:71
  299.3 5.4 %collective-permute-start.24 = (f32[20,8,8,1]{0,3,2,1:T(1,128)S(1)}, f32[20,8,8,1]{0,3,2,1:T(1,128)S(1)}, u32[]{:S(2)}, u32[]{:S(2)}) collective-permute-start(f32[20,8,8,1]{0,3,2,1:T(1,128)S(1)} %get-tuple-element.74), channel_id=1, source_target_pairs={{0,1},{1,2},{2,3},{3,4},{4,5},{5,6},{6,7},{7,0},{8,9},{9,10},{10,1... | collective-permute-start | bytes 15368 | tf_op jit(solution)/shard_map/ppermute | solution.py:18
  307.7 3.4 collective-permute-start.26
  311.1 3.7 collective-permute-done.26
  318.8 9.0 %collective-permute-done.28 = f32[20,10,1,10]{0,3,2,1:T(8,128)S(1)} collective-permute-done((f32[20,10,1,10]{0,3,2,1:T(8,128)S(1)}, f32[20,10,1,10]{0,3,2,1:T(8,128)S(1)}, u32[]{:S(2)}, u32[]{:S(2)}) %collective-permute-start.28) | collective-permute-done | bytes 8032 | tf_op jit(solution)/shard_map/ppermute | solution.py:18
  421.6 3.3 gather_fusion.31
  438.8 3.8 compare_select_fusion.58
  444.6 5.5 %collective-permute-start.7 = (s32[1,64]{1,0:T(1,128)S(1)}, s32[1,64]{1,0:T(1,128)S(1)}, u32[]{:S(2)}, u32[]{:S(2)}) collective-permute-start(s32[1,64]{1,0:T(1,128)S(1)} %get-tuple-element.173), channel_id=1, source_target_pairs={{32,0},{64,32},{96,64},{128,96},{160,128},{192,160},{224,192},{256... | collective-permute-start | bytes 776 | tf_op jit(solution)/shard_map/ppermute | solution.py:29
  451.3 7.9 %collective-permute-start.9 = (s32[1,64]{1,0:T(1,128)S(1)}, s32[1,64]{1,0:T(1,128)S(1)}, u32[]{:S(2)}, u32[]{:S(2)}) collective-permute-start(s32[1,64]{1,0:T(1,128)S(1)} %get-tuple-element.171), channel_id=1, source_target_pairs={{8,0},{16,8},{24,16},{9,1},{17,9},{25,17},{10,2},{18,10},{26,18},{... | collective-permute-start | bytes 776 | tf_op jit(solution)/shard_map/ppermute | solution.py:29
  459.2 7.5 %collective-permute-start.10 = (s32[1,64]{1,0:T(1,128)S(1)}, s32[1,64]{1,0:T(1,128)S(1)}, u32[]{:S(2)}, u32[]{:S(2)}) collective-permute-start(s32[1,64]{1,0:T(1,128)S(1)} %get-tuple-element.170), channel_id=1, source_target_pairs={{0,1},{1,2},{2,3},{3,4},{4,5},{5,6},{6,7},{7,0},{8,9},{9,10},{10,1... | collective-permute-start | bytes 776 | tf_op jit(solution)/shard_map/ppermute | solution.py:34
  468.8 4.7 collective-permute-done.11
  473.6 3.6 collective-permute-start.31
  478.5 7.9 %collective-permute-start.33 = (f32[21,64]{1,0:T(8,128)S(1)}, f32[21,64]{1,0:T(8,128)S(1)}, u32[]{:S(2)}, u32[]{:S(2)}) collective-permute-start(f32[21,64]{1,0:T(8,128)S(1)} %get-tuple-element.79), channel_id=1, source_target_pairs={{8,0},{16,8},{24,16},{9,1},{17,9},{25,17},{10,2},{18,10},{26,18},{... | collective-permute-start | bytes 16136 | tf_op jit(solution)/shard_map/ppermute | solution.py:29
  491.3 4.8 collective-permute-done.35
  497.2 12.9 %scatter_custom_fusion.3 = f32[512]{0:T(512)S(1)} fusion(s32[1792]{0:T(1024)S(1)} %pad_add_fusion.1, f32[1792]{0:T(1024)S(1)} %pad_maximum_fusion.26, f32[]{:T(128)} %constant.305.clone.1), kind=kCustom, calls=%fused_computation.548 | custom fusion | flops 1792 | bytes 2052 | tf_op jit(solution)/shard_map/scatter-add | solution.py:72
  510.1 12.4 %scatter_custom_fusion.2 = f32[512,20]{1,0:T(8,128)S(1)} fusion(s32[1792]{0:T(1024)S(1)} %pad_add_fusion.1, f32[1792,20]{1,0:T(8,128)S(1)} %copy.273, f32[]{:T(128)} %constant.263.clone.1), kind=kCustom, calls=%fused_computation.143 | custom fusion | flops 35840 | bytes 40964 | tf_op jit(solution)/shard_map/scatter-add | solution.py:71
  (483 shorter events, 290.0 us)
Async XLA Ops:
  32.3 49.8 %collective-permute-start = (s32[2,64]{0,1:T(8,128)S(1)}, s32[2,64]{0,1:T(8,128)S(1)}, u32[]{:S(2)}, u32[]{:S(2)}) collective-permute-start(s32[2,64]{0,1:T(8,128)S(1)} %get-tuple-element.69), channel_id=1, source_target_pairs={{0,32},{32,64},{64,96},{96,128},{128,160},{160,192},{192,224},{224... | collective-permute-start | bytes 1544 | tf_op jit(solution)/shard_map/ppermute | solution.py:29
  35.5 48.6 %collective-permute-start.1 = (s32[2,64]{0,1:T(8,128)S(1)}, s32[2,64]{0,1:T(8,128)S(1)}, u32[]{:S(2)}, u32[]{:S(2)}) collective-permute-start(s32[2,64]{0,1:T(8,128)S(1)} %get-tuple-element.65), channel_id=1, source_target_pairs={{32,0},{64,32},{96,64},{128,96},{160,128},{192,160},{224,192},{256... | collective-permute-start | bytes 1544 | tf_op jit(solution)/shard_map/ppermute | solution.py:29
  39.7 46.6 %collective-permute-start.2 = (s32[2,64]{0,1:T(8,128)S(1)}, s32[2,64]{0,1:T(8,128)S(1)}, u32[]{:S(2)}, u32[]{:S(2)}) collective-permute-start(s32[2,64]{0,1:T(8,128)S(1)} %get-tuple-element.66), channel_id=1, source_target_pairs={{0,8},{8,16},{16,24},{1,9},{9,17},{17,25},{2,10},{10,18},{18,26},{... | collective-permute-start | bytes 1544 | tf_op jit(solution)/shard_map/ppermute | solution.py:29
  41.0 50.6 %collective-permute-start.3 = (s32[2,64]{0,1:T(8,128)S(1)}, s32[2,64]{0,1:T(8,128)S(1)}, u32[]{:S(2)}, u32[]{:S(2)}) collective-permute-start(s32[2,64]{0,1:T(8,128)S(1)} %get-tuple-element.67), channel_id=1, source_target_pairs={{8,0},{16,8},{24,16},{9,1},{17,9},{25,17},{10,2},{18,10},{26,18},{... | collective-permute-start | bytes 1544 | tf_op jit(solution)/shard_map/ppermute | solution.py:29
  48.9 42.8 %collective-permute-start.4 = (s32[2,64]{0,1:T(8,128)S(1)}, s32[2,64]{0,1:T(8,128)S(1)}, u32[]{:S(2)}, u32[]{:S(2)}) collective-permute-start(s32[2,64]{0,1:T(8,128)S(1)} %get-tuple-element.68), channel_id=1, source_target_pairs={{0,1},{1,2},{2,3},{3,4},{4,5},{5,6},{6,7},{7,0},{8,9},{9,10},{10,1... | collective-permute-start | bytes 1544 | tf_op jit(solution)/shard_map/ppermute | solution.py:34
  82.1 9.7 %collective-permute-start.5 = (s32[2,64]{0,1:T(8,128)S(1)}, s32[2,64]{0,1:T(8,128)S(1)}, u32[]{:S(2)}, u32[]{:S(2)}) collective-permute-start(s32[2,64]{0,1:T(8,128)S(1)} %get-tuple-element.64), channel_id=1, source_target_pairs={{0,7},{1,0},{2,1},{3,2},{4,3},{5,4},{6,5},{7,6},{8,15},{9,8},{10,9... | collective-permute-start | bytes 1544 | tf_op jit(solution)/shard_map/ppermute | solution.py:34
  84.1 22.4 %collective-permute-start.13 = (f32[21,8,8,1]{0,3,2,1:T(1,128)S(1)}, f32[21,8,8,1]{0,3,2,1:T(1,128)S(1)}, u32[]{:S(2)}, u32[]{:S(2)}) collective-permute-start(f32[21,8,8,1]{0,3,2,1:T(1,128)S(1)} %get-tuple-element.63), channel_id=1, source_target_pairs={{1,0},{2,1},{3,2},{4,3},{5,4},{6,5},{7,6},{0,7},{9,8},{10,9},{11,1... | collective-permute-start | bytes 16136 | tf_op jit(solution)/shard_map/ppermute | solution.py:21
  86.3 20.2 %collective-permute-start.12 = (f32[21,8,8,1]{0,3,2,1:T(1,128)S(1)}, f32[21,8,8,1]{0,3,2,1:T(1,128)S(1)}, u32[]{:S(2)}, u32[]{:S(2)}) collective-permute-start(f32[21,8,8,1]{0,3,2,1:T(1,128)S(1)} %get-tuple-element.62), channel_id=1, source_target_pairs={{0,1},{1,2},{2,3},{3,4},{4,5},{5,6},{6,7},{7,0},{8,9},{9,10},{10,1... | collective-permute-start | bytes 16136 | tf_op jit(solution)/shard_map/ppermute | solution.py:18
  109.1 7.1 %collective-permute-start.14 = (f32[21,1,8,10]{0,3,2,1:T(8,128)S(1)}, f32[21,1,8,10]{0,3,2,1:T(8,128)S(1)}, u32[]{:S(2)}, u32[]{:S(2)}) collective-permute-start(f32[21,1,8,10]{0,3,2,1:T(8,128)S(1)} %get-tuple-element.60), channel_id=1, source_target_pairs={{0,32},{32,64},{64,96},{96,128},{128,160},{160,192},{192,224},{224... | collective-permute-start | bytes 20168 | tf_op jit(solution)/shard_map/ppermute | solution.py:18
  116.4 7.5 %collective-permute-start.17 = (f32[21,10,1,10]{0,3,2,1:T(8,128)S(1)}, f32[21,10,1,10]{0,3,2,1:T(8,128)S(1)}, u32[]{:S(2)}, u32[]{:S(2)}) collective-permute-start(f32[21,10,1,10]{0,3,2,1:T(8,128)S(1)} %get-tuple-element.59), channel_id=1, source_target_pairs={{8,0},{16,8},{24,16},{9,1},{17,9},{25,17},{10,2},{18,10},{26,18},{... | collective-permute-start | bytes 25208 | tf_op jit(solution)/shard_map/ppermute | solution.py:21
  121.6 13.0 %collective-permute-start.16 = (f32[21,10,1,10]{0,3,2,1:T(8,128)S(1)}, f32[21,10,1,10]{0,3,2,1:T(8,128)S(1)}, u32[]{:S(2)}, u32[]{:S(2)}) collective-permute-start(f32[21,10,1,10]{0,3,2,1:T(8,128)S(1)} %get-tuple-element.58), channel_id=1, source_target_pairs={{0,8},{8,16},{16,24},{1,9},{9,17},{17,25},{2,10},{10,18},{18,26},{... | collective-permute-start | bytes 25208 | tf_op jit(solution)/shard_map/ppermute | solution.py:18
  235.0 23.1 %collective-permute-start.18 = (f32[24,64]{1,0:T(8,128)S(1)}, f32[24,64]{1,0:T(8,128)S(1)}, u32[]{:S(2)}, u32[]{:S(2)}) collective-permute-start(f32[24,64]{1,0:T(8,128)S(1)} %get-tuple-element.87), channel_id=1, source_target_pairs={{0,32},{32,64},{64,96},{96,128},{128,160},{160,192},{192,224},{224... | collective-permute-start | bytes 18440 | tf_op jit(solution)/shard_map/ppermute | solution.py:29
  237.6 23.1 %collective-permute-start.19 = (f32[24,64]{1,0:T(8,128)S(1)}, f32[24,64]{1,0:T(8,128)S(1)}, u32[]{:S(2)}, u32[]{:S(2)}) collective-permute-start(f32[24,64]{1,0:T(8,128)S(1)} %get-tuple-element.83), channel_id=1, source_target_pairs={{32,0},{64,32},{96,64},{128,96},{160,128},{192,160},{224,192},{256... | collective-permute-start | bytes 18440 | tf_op jit(solution)/shard_map/ppermute | solution.py:29
  243.2 17.5 %collective-permute-start.20 = (f32[24,64]{1,0:T(8,128)S(1)}, f32[24,64]{1,0:T(8,128)S(1)}, u32[]{:S(2)}, u32[]{:S(2)}) collective-permute-start(f32[24,64]{1,0:T(8,128)S(1)} %get-tuple-element.84), channel_id=1, source_target_pairs={{0,8},{8,16},{16,24},{1,9},{9,17},{17,25},{2,10},{10,18},{18,26},{... | collective-permute-start | bytes 18440 | tf_op jit(solution)/shard_map/ppermute | solution.py:29
  244.5 16.2 %collective-permute-start.21 = (f32[24,64]{1,0:T(8,128)S(1)}, f32[24,64]{1,0:T(8,128)S(1)}, u32[]{:S(2)}, u32[]{:S(2)}) collective-permute-start(f32[24,64]{1,0:T(8,128)S(1)} %get-tuple-element.85), channel_id=1, source_target_pairs={{8,0},{16,8},{24,16},{9,1},{17,9},{25,17},{10,2},{18,10},{26,18},{... | collective-permute-start | bytes 18440 | tf_op jit(solution)/shard_map/ppermute | solution.py:29
  252.4 8.3 %collective-permute-start.22 = (f32[24,64]{1,0:T(8,128)S(1)}, f32[24,64]{1,0:T(8,128)S(1)}, u32[]{:S(2)}, u32[]{:S(2)}) collective-permute-start(f32[24,64]{1,0:T(8,128)S(1)} %get-tuple-element.86), channel_id=1, source_target_pairs={{0,1},{1,2},{2,3},{3,4},{4,5},{5,6},{6,7},{7,0},{8,9},{9,10},{10,1... | collective-permute-start | bytes 18440 | tf_op jit(solution)/shard_map/ppermute | solution.py:34
  258.2 6.8 %collective-permute-start.23 = (f32[24,64]{1,0:T(8,128)S(1)}, f32[24,64]{1,0:T(8,128)S(1)}, u32[]{:S(2)}, u32[]{:S(2)}) collective-permute-start(f32[24,64]{1,0:T(8,128)S(1)} %get-tuple-element.82), channel_id=1, source_target_pairs={{0,7},{1,0},{2,1},{3,2},{4,3},{5,4},{6,5},{7,6},{8,15},{9,8},{10,9... | collective-permute-start | bytes 18440 | tf_op jit(solution)/shard_map/ppermute | solution.py:34
  297.4 8.3 %collective-permute-start.25 = (f32[20,8,8,1]{0,3,2,1:T(1,128)S(1)}, f32[20,8,8,1]{0,3,2,1:T(1,128)S(1)}, u32[]{:S(2)}, u32[]{:S(2)}) collective-permute-start(f32[20,8,8,1]{0,3,2,1:T(1,128)S(1)} %get-tuple-element.75), channel_id=1, source_target_pairs={{1,0},{2,1},{3,2},{4,3},{5,4},{6,5},{7,6},{0,7},{9,8},{10,9},{11,1... | collective-permute-start | bytes 15368 | tf_op jit(solution)/shard_map/ppermute | solution.py:21
  299.3 6.5 %collective-permute-start.24 = (f32[20,8,8,1]{0,3,2,1:T(1,128)S(1)}, f32[20,8,8,1]{0,3,2,1:T(1,128)S(1)}, u32[]{:S(2)}, u32[]{:S(2)}) collective-permute-start(f32[20,8,8,1]{0,3,2,1:T(1,128)S(1)} %get-tuple-element.74), channel_id=1, source_target_pairs={{0,1},{1,2},{2,3},{3,4},{4,5},{5,6},{6,7},{7,0},{8,9},{9,10},{10,1... | collective-permute-start | bytes 15368 | tf_op jit(solution)/shard_map/ppermute | solution.py:18
  307.7 7.1 %collective-permute-start.26 = (f32[20,1,8,10]{0,3,2,1:T(8,128)S(1)}, f32[20,1,8,10]{0,3,2,1:T(8,128)S(1)}, u32[]{:S(2)}, u32[]{:S(2)}) collective-permute-start(f32[20,1,8,10]{0,3,2,1:T(8,128)S(1)} %get-tuple-element.72), channel_id=1, source_target_pairs={{0,32},{32,64},{64,96},{96,128},{128,160},{160,192},{192,224},{224... | collective-permute-start | bytes 19208 | tf_op jit(solution)/shard_map/ppermute | solution.py:18
  316.4 11.4 %collective-permute-start.28 = (f32[20,10,1,10]{0,3,2,1:T(8,128)S(1)}, f32[20,10,1,10]{0,3,2,1:T(8,128)S(1)}, u32[]{:S(2)}, u32[]{:S(2)}) collective-permute-start(f32[20,10,1,10]{0,3,2,1:T(8,128)S(1)} %get-tuple-element.70), channel_id=1, source_target_pairs={{0,8},{8,16},{16,24},{1,9},{9,17},{17,25},{2,10},{10,18},{18,26},{... | collective-permute-start | bytes 24008 | tf_op jit(solution)/shard_map/ppermute | solution.py:18
  436.9 52.4 %collective-permute-start.30 = (f32[21,64]{1,0:T(8,128)S(1)}, f32[21,64]{1,0:T(8,128)S(1)}, u32[]{:S(2)}, u32[]{:S(2)}) collective-permute-start(f32[21,64]{1,0:T(8,128)S(1)} %get-tuple-element.81), channel_id=1, source_target_pairs={{0,32},{32,64},{64,96},{96,128},{128,160},{160,192},{192,224},{224... | collective-permute-start | bytes 16136 | tf_op jit(solution)/shard_map/ppermute | solution.py:29
  442.6 16.6 %collective-permute-start.6 = (s32[1,64]{1,0:T(1,128)S(1)}, s32[1,64]{1,0:T(1,128)S(1)}, u32[]{:S(2)}, u32[]{:S(2)}) collective-permute-start(s32[1,64]{1,0:T(1,128)S(1)} %get-tuple-element.174), channel_id=1, source_target_pairs={{0,32},{32,64},{64,96},{96,128},{128,160},{160,192},{192,224},{224... | collective-permute-start | bytes 776 | tf_op jit(solution)/shard_map/ppermute | solution.py:29
  444.6 22.2 %collective-permute-start.7 = (s32[1,64]{1,0:T(1,128)S(1)}, s32[1,64]{1,0:T(1,128)S(1)}, u32[]{:S(2)}, u32[]{:S(2)}) collective-permute-start(s32[1,64]{1,0:T(1,128)S(1)} %get-tuple-element.173), channel_id=1, source_target_pairs={{32,0},{64,32},{96,64},{128,96},{160,128},{192,160},{224,192},{256... | collective-permute-start | bytes 776 | tf_op jit(solution)/shard_map/ppermute | solution.py:29
  450.0 18.7 %collective-permute-start.8 = (s32[1,64]{1,0:T(1,128)S(1)}, s32[1,64]{1,0:T(1,128)S(1)}, u32[]{:S(2)}, u32[]{:S(2)}) collective-permute-start(s32[1,64]{1,0:T(1,128)S(1)} %get-tuple-element.172), channel_id=1, source_target_pairs={{0,8},{8,16},{16,24},{1,9},{9,17},{17,25},{2,10},{10,18},{18,26},{... | collective-permute-start | bytes 776 | tf_op jit(solution)/shard_map/ppermute | solution.py:29
  451.3 17.4 %collective-permute-start.9 = (s32[1,64]{1,0:T(1,128)S(1)}, s32[1,64]{1,0:T(1,128)S(1)}, u32[]{:S(2)}, u32[]{:S(2)}) collective-permute-start(s32[1,64]{1,0:T(1,128)S(1)} %get-tuple-element.171), channel_id=1, source_target_pairs={{8,0},{16,8},{24,16},{9,1},{17,9},{25,17},{10,2},{18,10},{26,18},{... | collective-permute-start | bytes 776 | tf_op jit(solution)/shard_map/ppermute | solution.py:29
  459.2 9.5 %collective-permute-start.10 = (s32[1,64]{1,0:T(1,128)S(1)}, s32[1,64]{1,0:T(1,128)S(1)}, u32[]{:S(2)}, u32[]{:S(2)}) collective-permute-start(s32[1,64]{1,0:T(1,128)S(1)} %get-tuple-element.170), channel_id=1, source_target_pairs={{0,1},{1,2},{2,3},{3,4},{4,5},{5,6},{6,7},{7,0},{8,9},{9,10},{10,1... | collective-permute-start | bytes 776 | tf_op jit(solution)/shard_map/ppermute | solution.py:34
  466.8 6.7 %collective-permute-start.11 = (s32[1,64]{1,0:T(1,128)S(1)}, s32[1,64]{1,0:T(1,128)S(1)}, u32[]{:S(2)}, u32[]{:S(2)}) collective-permute-start(s32[1,64]{1,0:T(1,128)S(1)} %get-tuple-element.169), channel_id=1, source_target_pairs={{0,7},{1,0},{2,1},{3,2},{4,3},{5,4},{6,5},{7,6},{8,15},{9,8},{10,9... | collective-permute-start | bytes 776 | tf_op jit(solution)/shard_map/ppermute | solution.py:34
  473.6 17.6 %collective-permute-start.31 = (f32[21,64]{1,0:T(8,128)S(1)}, f32[21,64]{1,0:T(8,128)S(1)}, u32[]{:S(2)}, u32[]{:S(2)}) collective-permute-start(f32[21,64]{1,0:T(8,128)S(1)} %get-tuple-element.77), channel_id=1, source_target_pairs={{32,0},{64,32},{96,64},{128,96},{160,128},{192,160},{224,192},{256... | collective-permute-start | bytes 16136 | tf_op jit(solution)/shard_map/ppermute | solution.py:29
  477.2 14.0 %collective-permute-start.32 = (f32[21,64]{1,0:T(8,128)S(1)}, f32[21,64]{1,0:T(8,128)S(1)}, u32[]{:S(2)}, u32[]{:S(2)}) collective-permute-start(f32[21,64]{1,0:T(8,128)S(1)} %get-tuple-element.78), channel_id=1, source_target_pairs={{0,8},{8,16},{16,24},{1,9},{9,17},{17,25},{2,10},{10,18},{18,26},{... | collective-permute-start | bytes 16136 | tf_op jit(solution)/shard_map/ppermute | solution.py:29
  478.5 12.7 %collective-permute-start.33 = (f32[21,64]{1,0:T(8,128)S(1)}, f32[21,64]{1,0:T(8,128)S(1)}, u32[]{:S(2)}, u32[]{:S(2)}) collective-permute-start(f32[21,64]{1,0:T(8,128)S(1)} %get-tuple-element.79), channel_id=1, source_target_pairs={{8,0},{16,8},{24,16},{9,1},{17,9},{25,17},{10,2},{18,10},{26,18},{... | collective-permute-start | bytes 16136 | tf_op jit(solution)/shard_map/ppermute | solution.py:29
  489.3 6.8 %collective-permute-start.35 = (f32[21,64]{1,0:T(8,128)S(1)}, f32[21,64]{1,0:T(8,128)S(1)}, u32[]{:S(2)}, u32[]{:S(2)}) collective-permute-start(f32[21,64]{1,0:T(8,128)S(1)} %get-tuple-element.76), channel_id=1, source_target_pairs={{0,7},{1,0},{2,1},{3,2},{4,3},{5,4},{6,5},{7,6},{8,15},{9,8},{10,9... | collective-permute-start | bytes 16136 | tf_op jit(solution)/shard_map/ppermute | solution.py:34
  (105 other events, 446.2 us)
where the time goes:
time: 531 us; the launch traced here: 524 us
  local copies, waits for them, and re-layouts  215 us (40%)
  starting transfers between devices  129 us (24%)
  other arithmetic  110 us (21%)
  waiting for transfers between devices  41.1 us (8%)
  between operations  24.6 us (5%)
    gather x108, local copies, waits for them, and re-layouts, interpolate(): jnp.take(flat_field, base_index + flat_shift, axis=1)  182 us
    ppermute x16, starting transfers between devices, shifted(): return lax.ppermute(block, axis, route)  64.6 us
    scatter-add x2, other arithmetic, cell_average(): weights_sum = jax.ops.segment_sum(masses, cells, num_segments=ncells)  34.4 us
    ppermute x8, starting transfers between devices, from_behind(): return lax.ppermute(x, axis, [(i, (i + by) % size) for i in range(size)])  29 us
    ppermute x6, waiting for transfers between devices, extended_2(): lax.ppermute(lax.slice_in_dim(block, block.shape[dim] - width, None, axis...  27.3 us
    scatter-add x2, other arithmetic, cell_average(): jax.ops.segment_sum((values * masses[None, :]).T, cells, num_segments=nce...  21.9 us
    ppermute x6, starting transfers between devices, extended_2(): lax.ppermute(lax.slice_in_dim(block, block.shape[dim] - width, None, axis...  19.8 us
    ppermute x6, starting transfers between devices, extended_2(): lax.ppermute(lax.slice_in_dim(block, 0, width, axis=dim), axis, backward)  15.2 us
  transfers between devices with their start and end apart: 36, of which 8 were waited for; matrix products, arithmetic and copies ran while one was open for 8% of the time, Pallas kernels for 0%

commit v1 on v0

v1 whole, which is shorter than its diff:
```python
import functools

import jax
import jax.numpy as jnp
from jax import lax
from jax.experimental import pallas as pl
from jax.experimental.pallas import tpu as pltpu
from jax.sharding import PartitionSpec as P

MESH = pl.DeviceIdType.MESH
F32 = jnp.float32
BF16 = jnp.bfloat16

IEM_FACTOR = 0.4
TIME_STEP = 0.4
PRIOR_MASS = 2.0

ROWS = 24
LANES = 32
SIDE = 8
PLANE = 64
BLOCK = 64

NAMES = [
    "scalars",
    "particle_mass",
    "cell_first",
    "cell_second",
    "cell_final",
    "offset_first",
    "offset_second",
    "face_first",
    "face_second",
    "mean_field",
    "mix_rate",
    "react_in",
    "hidden_bias",
    "react_out",
]
INPUTS = len(NAMES)
ORDER = ["mean_field", "mix_rate", "cell_first", "offset_first", "react_in", "hidden_bias"]
ORDER += ["react_out", "face_first", "face_second", "cell_second", "cell_final"]
ORDER += ["particle_mass", "offset_second", "scalars"]

MOVE_STEPS = [(1, 0, 0), (-1, 0, 0), (0, 1, 0), (0, -1, 0), (0, 0, 1), (0, 0, -1)]

OWN = [slice(i, i + 256) for i in range(0, 1024, 256)]
NEW = [slice(0, 256), slice(256, 384)]

NT = (((1,), (1,)), ((), ()))


def dot(a, b):
    return jnp.dot(a, b, preferred_element_type=F32)


def dot_nt(a, b):
    return lax.dot_general(a, b, NT, preferred_element_type=F32)


def parts(v):
    high = v.astype(BF16)
    return high, (v - high.astype(F32)).astype(BF16)


def parts_wide(v):
    high = v.astype(BF16).astype(F32)
    return high, v - high


def iota(shape, dim):
    return lax.broadcasted_iota(jnp.int32, shape, dim)


def spline(u):
    return 0.5 * (0.5 - u) ** 2, 0.75 - u * u, 0.5 * (0.5 + u) ** 2


def along(cell, offset, low_ok, high_ok):
    low, mid, high = spline(offset)
    away = iota((SIDE, cell.shape[1]), 0) - cell
    inner = jnp.where(
        away == 0, mid, jnp.where(away == 1, high, jnp.where(away == -1, low, 0.0))
    )
    return (
        inner,
        jnp.where(cell == 0, low, 0.0) * low_ok,
        jnp.where(cell == SIDE - 1, high, 0.0) * high_ok,
    )


def weights(cells, offsets, ok):
    x_in, x_low, x_high = along(cells >> 6, offsets[0], ok[0], ok[1])
    y_in, y_low, y_high = along((cells >> 3) & 7, offsets[1], ok[2], ok[3])
    z_in, z_low, z_high = along(cells & 7, offsets[2], 1.0, 1.0)
    inner = jnp.concatenate([z_in * y_in[y : y + 1] for y in range(SIDE)], axis=0)
    row = iota(z_in.shape, 0)
    corner = jnp.where(
        row == 0,
        y_low * z_low,
        jnp.where(
            row == 1,
            y_low * z_high,
            jnp.where(row == 2, y_high * z_low, jnp.where(row == 3, y_high * z_high, 0.0)),
        ),
    )
    outer = jnp.concatenate(
        [z_in * y_low, z_in * y_high, y_in * z_low, y_in * z_high, corner, jnp.zeros_like(corner)],
        axis=0,
    )
    none = jnp.zeros((PLANE - outer.shape[0], cells.shape[1]), BF16)
    high, low = parts(outer)
    outer = jnp.concatenate([high, none, high, none, low, none], axis=0)
    return three_parts(*parts(inner)), outer, x_in, x_low, x_high


def compact(field):
    return jnp.concatenate([field[LANES * x : LANES * x + ROWS] for x in range(SIDE)], axis=0)


def spread(field):
    none = jnp.zeros((LANES - ROWS, field.shape[1]), field.dtype)
    pieces = []
    for x in range(SIDE):
        pieces += [field[ROWS * x : ROWS * (x + 1)], none]
    return jnp.concatenate(pieces, axis=0)


def three_parts(high, low):
    return jnp.concatenate([high, high, low], axis=0)


def left_of(field):
    high, low = parts_wide(field)
    return jnp.concatenate([high, low, high], axis=1).astype(BF16)


def left_outer(outer):
    high, low = parts_wide(outer)
    turned = jnp.concatenate([high, low], axis=0).T
    base = SIDE * LANES
    rows = jnp.concatenate(
        [
            compact(turned[:base]),
            turned[base + 3 * LANES : base + 3 * LANES + ROWS],
            turned[base : base + ROWS],
        ],
        axis=0,
    )
    return jnp.concatenate([rows, rows[:, :PLANE]], axis=1).astype(BF16)


def gather_own(result, x_in):
    total = x_in[0:1] * result[:ROWS]
    for x in range(1, SIDE):
        total = total + x_in[x : x + 1] * result[ROWS * x : ROWS * (x + 1)]
    return total


def gather_inner(left, w):
    return gather_own(dot(left, w[0]), w[2])


def gather_outer(lefts, w):
    result = dot(lefts[0], w[1])
    own = SIDE * ROWS
    sides = dot(lefts[1], w[0]) + result[own:]
    return gather_own(result[:own], w[2]) + w[3] * sides[:ROWS] + w[4] * sides[ROWS:]


def react(values, sampled, first, second):
    mixed = values - IEM_FACTOR * sampled[20:21] * (values - sampled)
    mixed = jnp.where(iota(mixed.shape, 0) == 20, 1.0, mixed)
    high, low = parts_wide(mixed)
    none = jnp.zeros((128 - 3 * ROWS, mixed.shape[1]), F32)
    stacked = jnp.concatenate([high, low, high, none], axis=0).astype(BF16)
    hidden_high, hidden_low = parts(jnp.tanh(dot(first, stacked)))
    result = dot(second, jnp.concatenate([hidden_high, hidden_low], axis=0))
    return mixed + TIME_STEP * (result[:ROWS] + result[ROWS:])


def slots_of(faces):
    count = faces.shape[1]
    code = iota((SIDE, count), 0)
    chosen = code + 1 == faces
    mask = jnp.where(chosen, 1.0, 0.0)
    chunks = count // 128
    stacked = jnp.concatenate(
        [mask[:, 128 * j : 128 * (j + 1)] for j in range(chunks)], axis=0
    ).astype(BF16)
    row, col = iota((128, 256), 0), iota((128, 256), 1)
    counter = jnp.where((row < col) | (col >= 128), 1.0, 0.0).astype(BF16)
    ranks = dot(stacked, counter)
    before = jnp.zeros((SIDE, 128), F32)
    pieces = []
    for j in range(chunks):
        rows = slice(SIDE * j, SIDE * (j + 1))
        pieces.append(ranks[rows, :128] + before)
        before = before + ranks[rows, 128:]
    rank = jnp.concatenate(pieces, axis=1)
    place = jnp.where(chosen, rank.astype(jnp.int32) + BLOCK * code + 1, 0)
    return jnp.sum(place, axis=0, keepdims=True) - 1


def one_hot(index, size):
    shape = (16, index.shape[1])
    away = iota(shape, 0).astype(F32).astype(BF16)
    away = away - jnp.broadcast_to(index.astype(F32), shape).astype(BF16)
    one, zero = jnp.ones(shape, BF16), jnp.zeros(shape, BF16)
    return jnp.concatenate(
        [jnp.where(away == jnp.full(shape, -16.0 * b, BF16), one, zero) for b in range(size // 16)],
        axis=0,
    )


def pack(payload, slots):
    high, low = parts_wide(payload)
    chosen = jnp.concatenate([one_hot(slots, 256), one_hot(slots - 256, 128)], axis=0)
    return dot_nt(jnp.concatenate([high, low], axis=0).astype(BF16), chosen)


def scatter(values, masses, cells):
    high, low = parts_wide(values * masses)
    stacked = jnp.concatenate([high, low], axis=0)
    upper = (cells >> 8).astype(F32)
    left = jnp.concatenate([stacked * (1.0 - upper), stacked * upper], axis=0)
    return dot_nt(left.astype(BF16), one_hot(cells & 255, 4 * PLANE))


def by_cell(result):
    pieces = []
    for x in range(SIDE):
        base = 2 * ROWS * (x // 4)
        lanes = slice(PLANE * (x % 4), PLANE * (x % 4 + 1))
        pieces.append(result[base : base + ROWS, lanes] + result[base + ROWS : base + 2 * ROWS, lanes])
    return jnp.concatenate(pieces, axis=0)


def average(sums, field):
    pieces = []
    for x in range(SIDE):
        rows = slice(ROWS * x, ROWS * (x + 1))
        one, old = sums[rows], field[rows]
        new = (one + PRIOR_MASS * old) / (one[20:21] + PRIOR_MASS)
        pieces.append(jnp.where(iota(new.shape, 0) == 20, old, new))
    return jnp.concatenate(pieces, axis=0)


def kernel(sizes, *refs):
    inputs, out_ref, refs = refs[:INPUTS], refs[INPUTS], refs[INPUTS + 1 :]
    local, refs = refs[:INPUTS], refs[INPUTS:]
    (
        plane,
        z_send,
        c_send,
        x_send,
        face_got,
        corner_got,
        edge_got,
        point_got,
        x_got,
        packed,
        got,
        rows_buf,
        pay,
        local_sem,
        halo_send_sem,
        halo_recv_sem,
        move_send_sem,
        move_recv_sem,
    ) = refs
    n_gx, n_gy, n_gz = sizes
    gx, gy, gz = lax.axis_index("gx"), lax.axis_index("gy"), lax.axis_index("gz")

    def three(index, size):
        return {-1: lax.rem(index + size - 1, size), 0: index, 1: lax.rem(index + 1, size)}

    near_x, near_y, near_z = three(gx, n_gx), three(gy, n_gy), three(gz, n_gz)

    def at(dx, dy, dz):
        return near_x[dx], near_y[dy], near_z[dz]

    faces = [(1, 0), (-1, 0), (0, 1), (0, -1)]
    corners = [(1, 1), (1, -1), (-1, 1), (-1, -1)]
    x_steps = [1, -1]
    halo_steps = [(0, dy, dz) for dy, dz in faces + corners]
    halo_steps += [(dx, dy, dz) for dx in x_steps for dy, dz in faces + corners]
    halo_steps += [(dx, 0, 0) for dx in x_steps]

    loads = {
        name: pltpu.make_async_copy(a, to, local_sem.at[i])
        for i, (name, a, to) in enumerate(zip(NAMES, inputs, local))
    }
    for name in ORDER[:2]:
        loads[name].start()
    barrier = pltpu.get_barrier_semaphore()
    for step in halo_steps:
        pl.semaphore_signal(barrier, inc=1, device_id=at(*step), device_id_type=MESH)
    for name in ORDER[2:]:
        loads[name].start()

    def load(name):
        loads[name].wait()
        return local[NAMES.index(name)]

    def remote(src, dst, send_sem, recv_sem, step):
        copy = pltpu.make_async_remote_copy(
            src_ref=src,
            dst_ref=dst,
            send_sem=send_sem,
            recv_sem=recv_sem,
            device_id=at(*step),
            device_id_type=MESH,
        )
        copy.start()
        return copy

    def put(h, value):
        plane[h, 0] = value[:, :128]
        plane[h, 1] = value[:, 128:]

    def send_halo(h, first, source, target):
        return [
            remote(
                src,
                dst,
                halo_send_sem.at[h, first + i],
                halo_recv_sem.at[h, first + i],
                halo_steps[first + i],
            )
            for i, (src, dst) in enumerate(zip(source, target))
        ]

    def send_x(h, field):
        x_send[h, 0, :, 0:PLANE] = field[7 * ROWS : 8 * ROWS]
        x_send[h, 1, :, 0:PLANE] = field[0:ROWS]
        return send_halo(h, 24, [x_send.at[h, k] for k in range(2)], [x_got.at[h, k] for k in range(2)])

    def send_plane(h):
        for z, slot in ((7, 0), (0, 1)):
            for half in range(2):
                z_send[h, slot, half] = plane[h, half, pl.ds(z, SIDE, stride=SIDE), :]
        for slot, row in enumerate((63, 56, 7, 0)):
            for half in range(2):
                c_send[h, slot, half] = plane[h, half, row : row + 1, :]
        rows = plane.at[h]
        source = [rows.at[:, 56:64], rows.at[:, 0:8], z_send.at[h, 0], z_send.at[h, 1]]
        source += [c_send.at[h, slot] for slot in range(4)]
        target = [face_got.at[h, slot] for slot in range(4)]
        target += [corner_got.at[h, slot] for slot in range(4)]
        for k, half in ((0, 1), (1, 0)):
            source += [rows.at[half, 56:64], rows.at[half, 0:8]]
            source += [z_send.at[h, slot, half] for slot in range(2)]
            source += [c_send.at[h, slot, half] for slot in range(4)]
            target += [edge_got.at[h, k, slot] for slot in range(4)]
            target += [point_got.at[h, k, slot] for slot in range(4)]
        return send_halo(h, 0, source, target)

    def stack_outer(face, corner):
        row = iota((SIDE, 128), 0)
        last = jnp.zeros((SIDE, 128), F32)
        for slot in range(4):
            last = jnp.where(row == slot, corner[slot], last)
        none = jnp.zeros((PLANE - 5 * SIDE, 128), F32)
        return jnp.concatenate(face + [last, none], axis=0)

    def halo(h, copies):
        for copy in copies:
            copy.wait_recv()
        both = [
            stack_outer(
                [face_got[h, slot, half] for slot in range(4)],
                [corner_got[h, slot, half] for slot in range(4)],
            )
            for half in range(2)
        ]
        side = [
            stack_outer(
                [edge_got[h, k, slot] for slot in range(4)],
                [point_got[h, k, slot] for slot in range(4)],
            )
            for k in range(2)
        ]
        last = jnp.where(iota((PLANE, 128), 1) < PLANE, side[1], side[0])
        planes = left_outer(jnp.concatenate(both + [last], axis=1))
        sides = jnp.concatenate([x_got[h, 0], x_got[h, 1]], axis=0)[:, :PLANE]
        return planes, left_of(sides)

    lower = iota((16, 128), 1) < BLOCK

    def turned(value):
        return pltpu.roll(value, BLOCK, 1)

    def send_moves(m, block):
        copies = []
        for t in (1, 0, 2):
            tile = block[:, 128 * t : 128 * (t + 1)]
            packed[m, 2 * t] = jnp.where(lower, tile[:16], turned(tile[16:]))
            packed[m, 2 * t + 1] = jnp.where(lower, turned(tile[:16]), tile[16:])
            for k in (2 * t, 2 * t + 1):
                copies.append(
                    remote(
                        packed.at[m, k],
                        got.at[m, k],
                        move_send_sem.at[m, k],
                        move_recv_sem.at[m, k],
                        MOVE_STEPS[k],
                    )
                )
        return copies

    def arrivals(m, copies):
        for copy in copies:
            copy.wait_recv()
        tiles = []
        for t in range(3):
            one, two = got[m, 2 * t], got[m, 2 * t + 1]
            top = jnp.where(lower, one, turned(two))
            bottom = jnp.where(lower, turned(one), two)
            tiles.append(jnp.concatenate([top, bottom], axis=0))
        return jnp.concatenate(tiles, axis=1)

    plane[0] = jnp.zeros((2, PLANE, 128), F32)
    x_send[...] = jnp.zeros(x_send.shape, F32)
    same_z = jnp.where(iota((PLANE, SIDE), 0) & 7 == iota((PLANE, SIDE), 1), 1.0, 0.0)
    same_y = iota((PLANE, PLANE), 0) >> 3 == iota((PLANE, PLANE), 1) & 7
    goes = (iota((PLANE, SIDE * LANES), 0) >> 3) * LANES + 20
    goes = jnp.where(iota((PLANE, SIDE * LANES), 1) == goes, 1.0, 0.0).astype(BF16)
    rate = jnp.zeros((PLANE, SIDE * LANES), F32)
    for part in parts(load("mix_rate")[...]):
        along_z = jnp.where(same_y, dot_nt(same_z.astype(BF16), part), 0.0)
        rate = rate + dot(along_z.astype(BF16), goes)
    mean_ref = load("mean_field")
    for x in range(SIDE):
        base = LANES * (x % 4)
        plane[0, x // 4, :, base : base + 20] = mean_ref[PLANE * x : PLANE * (x + 1), :]
    inner1 = jnp.concatenate([plane[0, 0], plane[0, 1]], axis=1) + rate
    put(0, inner1)

    pl.semaphore_wait(barrier, len(halo_steps))
    halo_copies1 = send_plane(0)
    field1 = compact(inner1.T)
    halo_copies1 = halo_copies1 + send_x(0, field1)

    ok = [
        jnp.where(gx > 0, 1.0, 0.0),
        jnp.where(gx < n_gx - 1, 1.0, 0.0),
        jnp.where(gy > 0, 1.0, 0.0),
        jnp.where(gy < n_gy - 1, 1.0, 0.0),
    ]

    cell1 = load("cell_first")
    off1 = load("offset_first")
    face1 = load("face_first")
    cell2 = load("cell_second")
    cell3 = load("cell_final")
    mass = load("particle_mass")
    off2 = load("offset_second")
    pay[0:20, :] = load("scalars")[...]
    pay[20:21, :] = mass[...]
    pay[21:24, :] = off2[...]
    pay[24:25, :] = cell2[...].astype(F32)
    pay[25:26, :] = cell3[...].astype(F32)
    pay[26:27, :] = cell1[...].astype(F32)
    pay[27:30, :] = off1[...]
    pay[30:32, :] = jnp.zeros((2, pay.shape[1]), F32)

    def packed_movers(faces):
        slots = slots_of(faces)
        block = sum(pack(pay[:, lanes], slots[:, lanes]) for lanes in OWN)
        return block[:32] + block[32:]

    def weights_at(cells, offsets, lanes):
        return weights(cells[:, lanes], [offsets[d : d + 1, lanes] for d in range(3)], ok)

    def scalars_of(block):
        row = iota((ROWS, block.shape[1]), 0)
        return jnp.where(row == 20, 1.0, jnp.where(row < 20, block[:ROWS], 0.0))

    def message(values, block):
        row = iota((ROWS, block.shape[1]), 0)
        return jnp.concatenate([jnp.where(row < 20, values, block[:ROWS]), block[ROWS:]], axis=0)

    def work(values, sampled, outer, w):
        return react(values, sampled + gather_outer(outer, w), first, second)

    movers = packed_movers(face1[...])
    mover_cells = movers[26:27].astype(jnp.int32)
    w_movers = [weights_at(mover_cells, movers[27:30], lanes) for lanes in NEW]

    left = left_of(field1)
    in_movers = [gather_inner(left, w) for w in w_movers]

    rows_buf[...] = jnp.zeros(rows_buf.shape, F32)
    rows_buf[0, 0:20, :] = load("react_in")[...]
    rows_buf[0, 20:21, :] = load("hidden_bias")[...]
    rows_buf[1, 0:20, :] = load("react_out")[...]
    high, low = parts_wide(rows_buf[0])
    first = jnp.concatenate(
        [high, high, low, jnp.zeros((128 - 3 * ROWS, 128), F32)], axis=0
    ).T.astype(BF16)
    high, low = parts_wide(rows_buf[1])
    second = jnp.concatenate(
        [
            jnp.concatenate([high, high], axis=1),
            jnp.concatenate([low, jnp.zeros_like(low)], axis=1),
        ],
        axis=0,
    ).astype(BF16)

    w_own, in_own = [], []
    for lanes in OWN:
        w_own.append(weights_at(cell1, off1, lanes))
        in_own.append(gather_inner(left, w_own[-1]))

    outer = halo(0, halo_copies1)
    moved = [
        message(work(scalars_of(movers[:, lanes]), one, outer, w), movers[:, lanes])
        for lanes, one, w in zip(NEW, in_movers, w_movers)
    ]
    move_copies1 = send_moves(0, jnp.concatenate(moved, axis=1))

    values, sums = [], 0.0
    for lanes, one, w in zip(OWN, in_own, w_own):
        values.append(work(scalars_of(pay[:, lanes]), one, outer, w))
        stay = jnp.where(face1[:, lanes] == 0, mass[:, lanes], 0.0)
        sums = sums + scatter(values[-1], stay, cell2[:, lanes])
        pay[0:20, lanes] = values[-1][:20]

    came = arrivals(0, move_copies1)
    lane = iota((1, 6 * BLOCK), 1)
    alive = jnp.where(
        lane < 64,
        ok[0],
        jnp.where(lane < 128, ok[1], jnp.where(lane < 192, ok[2], jnp.where(lane < 256, ok[3], 1.0))),
    )
    came_values = [scalars_of(came[:, lanes]) for lanes in NEW]
    came_mass = came[20:21] * alive
    came_cell2 = came[24:25].astype(jnp.int32)
    came_cell3 = came[25:26].astype(jnp.int32)
    for lanes, one in zip(NEW, came_values):
        sums = sums + scatter(one, came_mass[:, lanes], came_cell2[:, lanes])
    field2 = average(by_cell(sums), field1)
    put(1, spread(field2).T)
    halo_copies2 = send_plane(1) + send_x(1, field2)

    face2 = load("face_second")
    movers = packed_movers(face2[...])
    mover_cells = movers[24:25].astype(jnp.int32)
    w_movers = [weights_at(mover_cells, movers[21:24], lanes) for lanes in NEW]

    left = left_of(field2)
    in_movers = [gather_inner(left, w) for w in w_movers]
    w_own, in_own = [], []
    for lanes in OWN:
        w_own.append(weights_at(cell2, off2, lanes))
        in_own.append(gather_inner(left, w_own[-1]))
    w_came, in_came = [], []
    for lanes in NEW:
        w_came.append(weights_at(came_cell2, came[21:24], lanes))
        in_came.append(gather_inner(left, w_came[-1]))

    outer = halo(1, halo_copies2)
    moved = [
        message(work(scalars_of(movers[:, lanes]), one, outer, w), movers[:, lanes])
        for lanes, one, w in zip(NEW, in_movers, w_movers)
    ]
    move_copies2 = send_moves(1, jnp.concatenate(moved, axis=1))

    sums = 0.0
    for lanes, old, one, w in zip(OWN, values, in_own, w_own):
        new = work(old, one, outer, w)
        stay = jnp.where(face1[:, lanes] + face2[:, lanes] == 0, mass[:, lanes], 0.0)
        sums = sums + scatter(new, stay, cell3[:, lanes])
    for lanes, old, one, w in zip(NEW, came_values, in_came, w_came):
        new = work(old, one, outer, w)
        sums = sums + scatter(new, came_mass[:, lanes], came_cell3[:, lanes])

    last = arrivals(1, move_copies2)
    last_mass = last[20:21] * alive
    last_cell = last[25:26].astype(jnp.int32)
    for lanes in NEW:
        sums = sums + scatter(scalars_of(last[:, lanes]), last_mass[:, lanes], last_cell[:, lanes])
    sums = by_cell(sums)
    put(2, spread(average(sums, field2)).T)
    for x in range(SIDE):
        base = LANES * (x % 4)
        out_ref[PLANE * x : PLANE * (x + 1), :] = plane[2, x // 4, :, base : base + 20]

    for copy in halo_copies1 + move_copies1 + halo_copies2 + move_copies2:
        copy.wait_send()


def shards(
    sizes,
    scalars,
    particle_mass,
    cell_first,
    cell_second,
    cell_final,
    offset_first,
    offset_second,
    face_first,
    face_second,
    mean_field,
    mix_rate,
    react_in,
    hidden_bias,
    react_out,
):
    row = lambda a: a.reshape(1, -1)
    operands = [
        scalars,
        row(particle_mass),
        row(cell_first),
        row(cell_second),
        row(cell_final),
        offset_first,
        offset_second,
        row(face_first),
        row(face_second),
        mean_field.transpose(1, 2, 3, 0).reshape(SIDE * PLANE, 20),
        mix_rate.reshape(PLANE, SIDE),
        react_in.T,
        row(hidden_bias),
        react_out,
    ]
    operands = [pltpu.with_memory_space_constraint(a, pltpu.HBM) for a in operands]
    vmem = pl.BlockSpec(memory_space=pltpu.VMEM)
    result = pl.pallas_call(
        functools.partial(kernel, sizes),
        out_shape=jax.ShapeDtypeStruct((SIDE * PLANE, 20), F32),
        in_specs=[pl.BlockSpec(memory_space=pltpu.HBM)] * len(operands),
        out_specs=vmem,
        scratch_shapes=[pltpu.VMEM(a.shape, a.dtype) for a in operands]
        + [
            pltpu.VMEM((3, 2, PLANE, 128), F32),
            pltpu.VMEM((2, 2, 2, SIDE, 128), F32),
            pltpu.VMEM((2, 4, 2, 1, 128), F32),
            pltpu.VMEM((2, 2, ROWS, 128), F32),
            pltpu.VMEM((2, 4, 2, SIDE, 128), F32),
            pltpu.VMEM((2, 4, 2, 1, 128), F32),
            pltpu.VMEM((2, 2, 4, SIDE, 128), F32),
            pltpu.VMEM((2, 2, 4, 1, 128), F32),
            pltpu.VMEM((2, 2, ROWS, 128), F32),
            pltpu.VMEM((2, 6, 16, 128), F32),
            pltpu.VMEM((2, 6, 16, 128), F32),
            pltpu.VMEM((2, ROWS, 128), F32),
            pltpu.VMEM((32, 1024), F32),
            pltpu.SemaphoreType.DMA((INPUTS,)),
            pltpu.SemaphoreType.DMA((2, 26)),
            pltpu.SemaphoreType.DMA((2, 26)),
            pltpu.SemaphoreType.DMA((2, 6)),
            pltpu.SemaphoreType.DMA((2, 6)),
        ],
        compiler_params=pltpu.CompilerParams(
            collective_id=0, has_side_effects=True, vmem_limit_bytes=40 * 1024 * 1024
        ),
    )(*operands)
    return result.reshape(SIDE, SIDE, SIDE, 20).transpose(3, 0, 1, 2)


def solution(mesh):
    particles = P(("gx", "gy", "gz"))
    in_specs = (
        P(None, ("gx", "gy", "gz")),
        particles,
        particles,
        particles,
        particles,
        P(None, ("gx", "gy", "gz")),
        P(None, ("gx", "gy", "gz")),
        particles,
        particles,
        P(None, "gx", "gy", "gz"),
        P("gx", "gy", "gz"),
        P(),
        P(),
        P(),
    )
    sizes = (mesh.shape["gx"], mesh.shape["gy"], mesh.shape["gz"])
    return jax.shard_map(
        functools.partial(shards, sizes),
        mesh=mesh,
        in_specs=in_specs,
        out_specs=P(None, "gx", "gy", "gz"),
        check_vma=False,
    )
```

time: 531 us -> 46.4 us (0.09)
  the two profiles are of different devices: /device:TPU:483 before, /device:TPU:1 now
where the time goes in v1:
time: 46.4 us; the launch traced here: 46.3 us
  Pallas kernels  45.6 us (98%)
  local copies, waits for them, and re-layouts  0.71 us (2%)
    pallas_call x1, Pallas kernels, shards(): pl.pallas_call(functools.partial(kernel, sizes), out_shape=jax.ShapeDtype...  45.6 us

profile of v1, /device:TPU:1, one launch (start us, length us, event | category | flops | bytes accessed | tf_op | source)
XLA Modules:
  0.0 46.3 jit_solution(14623858672778910230)
XLA Ops:
  0.0 45.6 %shard_map.136 = f32[512,20]{1,0:T(8,128)S(1)} custom-call(f32[20,1024]{1,0:T(8,128)} %refs_0_.1, f32[1,1024]{1,0:T(1,128)} %bitcast.19, s32[1,1024]{1,0:T(1,128)} %bitcast.20, s32[1,1024]{1,0:T(1,128)} %bitcast.21, s32[1,1024]{1,0:T(1,128)} %bitcast.22, f32[3,1024]{1,0:T(4,128)} %refs_5_.1, f32[3,1024]{1,0:T(4,128)} %refs_6_.1, s32[1,1024]{1,0:T(1,128)} %bitcast.23, ...), custom_call_target="tpu_custom_call" | custom-call | tf_op jit(solution)/shard_map/pallas_call | solution.py:630
  45.6 0.7 %copy.16 = f32[20,8,8,8]{0,3,2,1:T(8,128)} copy(f32[20,8,8,8]{0,3,2,1:T(8,128)S(1)} %bitcast.15) | data formatting | bytes 81920

commit v2 on v1

v2 whole, which is shorter than its diff:
```python
import functools

import jax
import jax.numpy as jnp
from jax import lax
from jax.experimental import pallas as pl
from jax.experimental.pallas import tpu as pltpu
from jax.sharding import PartitionSpec as P

MESH = pl.DeviceIdType.MESH
F32 = jnp.float32
BF16 = jnp.bfloat16

IEM_FACTOR = 0.4
TIME_STEP = 0.4
PRIOR_MASS = 2.0

ROWS = 24
LANES = 32
SIDE = 8
PLANE = 64
BLOCK = 64

NAMES = [
    "scalars",
    "particle_mass",
    "cell_first",
    "cell_second",
    "cell_final",
    "offset_first",
    "offset_second",
    "face_first",
    "face_second",
    "mean_field",
    "mix_rate",
    "react_in",
    "hidden_bias",
    "react_out",
]
INPUTS = len(NAMES)
ORDER = ["mean_field", "mix_rate", "cell_first", "offset_first", "react_in", "hidden_bias"]
ORDER += ["react_out", "face_first", "face_second", "cell_second", "cell_final"]
ORDER += ["particle_mass", "offset_second", "scalars"]

MOVE_STEPS = [(1, 0, 0), (-1, 0, 0), (0, 0, 1), (0, 0, -1), (0, 1, 0), (0, -1, 0)]

OWN = [slice(i, i + 256) for i in range(0, 1024, 256)]
NEAR, FAR = slice(0, 256), slice(256, 384)

NT = (((1,), (1,)), ((), ()))


def dot(a, b):
    return jnp.dot(a, b, preferred_element_type=F32)


def dot_nt(a, b):
    return lax.dot_general(a, b, NT, preferred_element_type=F32)


def parts(v):
    high = v.astype(BF16)
    return high, (v - high.astype(F32)).astype(BF16)


def parts_wide(v):
    high = v.astype(BF16).astype(F32)
    return high, v - high


def iota(shape, dim):
    return lax.broadcasted_iota(jnp.int32, shape, dim)


def spline(u):
    return 0.5 * (0.5 - u) ** 2, 0.75 - u * u, 0.5 * (0.5 + u) ** 2


def along(cell, offset, low_ok, high_ok):
    low, mid, high = spline(offset)
    away = iota((SIDE, cell.shape[1]), 0) - cell
    inner = jnp.where(
        away == 0, mid, jnp.where(away == 1, high, jnp.where(away == -1, low, 0.0))
    )
    return (
        inner,
        jnp.where(cell == 0, low, 0.0) * low_ok,
        jnp.where(cell == SIDE - 1, high, 0.0) * high_ok,
    )


def weights(cells, offsets, ok):
    x_in, x_low, x_high = along(cells >> 6, offsets[0], ok[0], ok[1])
    y_in, y_low, y_high = along((cells >> 3) & 7, offsets[1], ok[2], ok[3])
    z_in, z_low, z_high = along(cells & 7, offsets[2], 1.0, 1.0)
    inner = jnp.concatenate([z_in * y_in[y : y + 1] for y in range(SIDE)], axis=0)
    row = iota(z_in.shape, 0)
    corner = jnp.where(
        row == 0,
        y_low * z_low,
        jnp.where(
            row == 1,
            y_low * z_high,
            jnp.where(row == 2, y_high * z_low, jnp.where(row == 3, y_high * z_high, 0.0)),
        ),
    )
    outer = jnp.concatenate(
        [z_in * y_low, z_in * y_high, y_in * z_low, y_in * z_high, corner, jnp.zeros_like(corner)],
        axis=0,
    )
    none = jnp.zeros((PLANE - outer.shape[0], cells.shape[1]), BF16)
    high, low = parts(outer)
    outer = jnp.concatenate([high, none, high, none, low, none], axis=0)
    return three_parts(*parts(inner)), outer, x_in, x_low, x_high


def compact(field):
    return jnp.concatenate([field[LANES * x : LANES * x + ROWS] for x in range(SIDE)], axis=0)


def spread(field):
    none = jnp.zeros((LANES - ROWS, field.shape[1]), field.dtype)
    pieces = []
    for x in range(SIDE):
        pieces += [field[ROWS * x : ROWS * (x + 1)], none]
    return jnp.concatenate(pieces, axis=0)


def three_parts(high, low):
    return jnp.concatenate([high, high, low], axis=0)


def left_of(field):
    high, low = parts_wide(field)
    return jnp.concatenate([high, low, high], axis=1).astype(BF16)


def left_outer(outer):
    high, low = parts_wide(outer)
    turned = jnp.concatenate([high, low], axis=0).T[: (SIDE + 2) * ROWS]
    return jnp.concatenate([turned, turned[:, :PLANE]], axis=1).astype(BF16)


def gather_own(result, x_in):
    total = x_in[0:1] * result[:ROWS]
    for x in range(1, SIDE):
        total = total + x_in[x : x + 1] * result[ROWS * x : ROWS * (x + 1)]
    return total


def gather(left, ws, which):
    results = [dot(left, w[which]) for w in ws]
    totals = []
    for result, w in zip(results, ws):
        sides = result[SIDE * ROWS :]
        own = gather_own(result, w[2])
        totals.append(own + w[3] * sides[:ROWS] + w[4] * sides[ROWS:])
    return totals


def mix(values, sampled):
    mixed = values - IEM_FACTOR * sampled[20:21] * (values - sampled)
    return jnp.where(iota(mixed.shape, 0) == 20, 1.0, mixed)


def first_operand(mixed):
    high, low = parts_wide(mixed)
    none = jnp.zeros((128 - 3 * ROWS, mixed.shape[1]), F32)
    return jnp.concatenate([high, low, high, none], axis=0).astype(BF16)


def react(values, sampled, first, second):
    mixed = [mix(one, sample) for one, sample in zip(values, sampled)]
    operands = [first_operand(one) for one in mixed]
    hidden = [dot(first, one) for one in operands]
    hidden = [jnp.concatenate(parts(jnp.tanh(one)), axis=0) for one in hidden]
    results = [dot(second, one) for one in hidden]
    return [one + TIME_STEP * (result[:ROWS] + result[ROWS:]) for one, result in zip(mixed, results)]


def slots_of(faces):
    count = faces.shape[1]
    code = iota((SIDE, count), 0)
    own_code = jnp.where(code < 2, code + 1, jnp.where(code < 4, code + 3, code - 1))
    chosen = (own_code == faces) & (code < 6)
    mask = jnp.where(chosen, 1.0, 0.0)
    chunks = count // 128
    stacked = jnp.concatenate(
        [mask[:, 128 * j : 128 * (j + 1)] for j in range(chunks)], axis=0
    ).astype(BF16)
    row, col = iota((128, 256), 0), iota((128, 256), 1)
    counter = jnp.where((row < col) | (col >= 128), 1.0, 0.0).astype(BF16)
    ranks = dot(stacked, counter)
    before = jnp.zeros((SIDE, 128), F32)
    pieces = []
    for j in range(chunks):
        rows = slice(SIDE * j, SIDE * (j + 1))
        pieces.append(ranks[rows, :128] + before)
        before = before + ranks[rows, 128:]
    rank = jnp.concatenate(pieces, axis=1)
    place = jnp.where(chosen, rank.astype(jnp.int32) + BLOCK * code + 1, 0)
    return jnp.sum(place, axis=0, keepdims=True) - 1


def one_hot(index, size):
    shape = (16, index.shape[1])
    away = iota(shape, 0).astype(F32).astype(BF16)
    away = away - jnp.broadcast_to(index.astype(F32), shape).astype(BF16)
    one, zero = jnp.ones(shape, BF16), jnp.zeros(shape, BF16)
    return jnp.concatenate(
        [jnp.where(away == jnp.full(shape, -16.0 * b, BF16), one, zero) for b in range(size // 16)],
        axis=0,
    )


def pack_operand(payload):
    return jnp.concatenate(parts_wide(payload), axis=0).astype(BF16)


def slots_hot(slots):
    return jnp.concatenate([one_hot(slots, 256), one_hot(slots - 256, 128)], axis=0)


def scatter_operand(values, masses, cells):
    high, low = parts_wide(values * masses)
    stacked = jnp.concatenate([high, low], axis=0)
    upper = (cells >> 8).astype(F32)
    return jnp.concatenate([stacked * (1.0 - upper), stacked * upper], axis=0).astype(BF16)


def scatter(group):
    hot = [one_hot(cells & 255, 4 * PLANE) for _, _, cells in group]
    left = [scatter_operand(*one) for one in group]
    return sum(dot_nt(a, b) for a, b in zip(left, hot))


def by_cell(result):
    pieces = []
    for x in range(SIDE):
        base = 2 * ROWS * (x // 4)
        lanes = slice(PLANE * (x % 4), PLANE * (x % 4 + 1))
        pieces.append(result[base : base + ROWS, lanes] + result[base + ROWS : base + 2 * ROWS, lanes])
    return jnp.concatenate(pieces, axis=0)


def average(sums, field):
    pieces = []
    for x in range(SIDE):
        rows = slice(ROWS * x, ROWS * (x + 1))
        one, old = sums[rows], field[rows]
        new = (one + PRIOR_MASS * old) / (one[20:21] + PRIOR_MASS)
        pieces.append(jnp.where(iota(new.shape, 0) == 20, old, new))
    return jnp.concatenate(pieces, axis=0)


def kernel(sizes, *refs):
    inputs, out_ref, refs = refs[:INPUTS], refs[INPUTS], refs[INPUTS + 1 :]
    local, refs = refs[:INPUTS], refs[INPUTS:]
    (
        plane,
        z_send,
        c_send,
        x_send,
        near_got,
        tile_got,
        row_got,
        x_got,
        packed,
        got,
        rows_buf,
        pay,
        local_sem,
        halo_send_sem,
        halo_recv_sem,
        move_send_sem,
        move_recv_sem,
    ) = refs
    n_gx, n_gy, n_gz = sizes
    gx, gy, gz = lax.axis_index("gx"), lax.axis_index("gy"), lax.axis_index("gz")

    def three(index, size):
        return {-1: lax.rem(index + size - 1, size), 0: index, 1: lax.rem(index + 1, size)}

    near_x, near_y, near_z = three(gx, n_gx), three(gy, n_gy), three(gz, n_gz)

    def at(dx, dy, dz):
        return near_x[dx], near_y[dy], near_z[dz]

    signs = (1, -1)
    y_steps = [(0, dy, 0) for dy in signs]
    near_steps = [(dx, 0, dz) for dz in signs for dx in signs]
    near_steps += [(0, 0, dz) for dz in signs]
    x_steps = [(dx, 0, 0) for dx in signs]
    halo_steps = near_steps + x_steps + y_steps

    barrier = pltpu.get_barrier_semaphore()
    for step in halo_steps:
        pl.semaphore_signal(barrier, inc=1, device_id=at(*step), device_id_type=MESH)
    loads = {
        name: pltpu.make_async_copy(a, to, local_sem.at[i])
        for i, (name, a, to) in enumerate(zip(NAMES, inputs, local))
    }
    for name in ORDER:
        loads[name].start()

    def load(name):
        loads[name].wait()
        return local[NAMES.index(name)]

    def remote_copy(src, dst, send_sem, recv_sem, step):
        return pltpu.make_async_remote_copy(
            src_ref=src,
            dst_ref=dst,
            send_sem=send_sem,
            recv_sem=recv_sem,
            device_id=at(*step),
            device_id_type=MESH,
        )

    def put(h, value):
        plane[h, 0] = value[:, :128]
        plane[h, 1] = value[:, 128:]

    def all_of(buffer, send_sem, recv_sem):
        return remote_copy(buffer, buffer, send_sem, recv_sem, (1, 0, 0))

    def halo_kind(h, kind):
        buffer = (x_got, near_got, tile_got, row_got)[kind].at[h]
        return all_of(buffer, halo_send_sem.at[h, kind], halo_recv_sem.at[h, kind])

    def send_halo(h, kind, steps, source, target):
        for step, src, dst in zip(steps, source, target):
            remote_copy(
                src, dst, halo_send_sem.at[h, kind], halo_recv_sem.at[h, kind], step
            ).start()

    def prepare_near(h, field):
        x_send[h, 0, :, 0:PLANE] = field[7 * ROWS : 8 * ROWS]
        x_send[h, 1, :, 0:PLANE] = field[0:ROWS]
        put(h, jnp.concatenate([field, jnp.zeros((64, PLANE), F32)], axis=0).T)
        for z, slot in ((7, 0), (0, 1)):
            for half in range(2):
                z_send[h, slot, half] = plane[h, half, pl.ds(z, SIDE, stride=SIDE), :]

    def send_near(h):
        source = [z_send.at[h, slot, half] for slot in range(2) for half in (1, 0)]
        target = [near_got.at[h, 4 + 2 * slot + k] for slot in range(2) for k in range(2)]
        source += [z_send.at[h, slot] for slot in range(2)]
        target += [near_got.at[h, 2 * slot : 2 * slot + 2] for slot in range(2)]
        send_halo(h, 1, near_steps, source, target)
        send_halo(h, 0, x_steps, [x_send.at[h, k] for k in range(2)], [x_got.at[h, k] for k in range(2)])

    def send_y(h, field):
        halo_kind(h, 0).wait_recv()
        sides = jnp.concatenate([x_got[h, 0], x_got[h, 1]], axis=0)[:, :PLANE]
        put(h + 2, jnp.concatenate([field, sides, jnp.zeros((16, PLANE), F32)], axis=0).T)
        rows = plane.at[h + 2]
        y_rows = (slice(56, 64), slice(0, 8))
        send_halo(h, 2, y_steps, [rows.at[:, y] for y in y_rows], [tile_got.at[h, k] for k in range(2)])
        halo_kind(h, 1).wait_recv()
        lane = iota((SIDE, 128), 1)
        outer = []
        for slot in range(2):
            low = pltpu.roll(near_got[h, 4 + 2 * slot], 24, 1)
            high = pltpu.roll(near_got[h, 5 + 2 * slot], 88, 1)
            second_half = jnp.where(
                lane < 64, near_got[h, 2 * slot + 1], jnp.where(lane < 88, low, high)
            )
            halves = (near_got[h, 2 * slot], second_half)
            outer.append(jnp.concatenate(halves, axis=1))
            for half in range(2):
                c_send[h, 0, 2 * slot + half] = halves[half][7:8]
                c_send[h, 1, 2 * slot + half] = halves[half][0:1]
        send_halo(h, 3, y_steps, [c_send.at[h, k] for k in range(2)], [row_got.at[h, k] for k in range(2)])
        return jnp.concatenate([left_of(field), left_of(sides)], axis=0), outer

    def outer_left(h, outer):
        for kind in (2, 3):
            halo_kind(h, kind).wait_recv()
        faces = [jnp.concatenate([tile_got[h, k, 0], tile_got[h, k, 1]], axis=1) for k in range(2)]
        row = iota((SIDE, 256), 0)
        last = jnp.zeros((SIDE, 256), F32)
        for k in range(2):
            for slot in range(2):
                one = [row_got[h, k, 2 * slot + half] for half in range(2)]
                last = jnp.where(row == 2 * k + slot, jnp.concatenate(one, axis=1), last)
        none = jnp.zeros((PLANE - 5 * SIDE, 256), F32)
        return left_outer(jnp.concatenate(faces + outer + [last, none], axis=0))

    lower = iota((16, 128), 1) < BLOCK

    def turned(value):
        return pltpu.roll(value, BLOCK, 1)

    def move_sems(m, first):
        return move_send_sem.at[m, first // 4], move_recv_sem.at[m, first // 4]

    def moves(m, first):
        return all_of(got.at[m, 4:6] if first else got.at[m, 0:4], *move_sems(m, first))

    def send_moves(m, first, block):
        for t in range(block.shape[1] // 128):
            tile = block[:, 128 * t : 128 * (t + 1)]
            k = first + 2 * t
            packed[m, k] = jnp.where(lower, tile[:16], turned(tile[16:]))
            packed[m, k + 1] = jnp.where(lower, turned(tile[:16]), tile[16:])
            for i in (k, k + 1):
                remote_copy(
                    packed.at[m, i], got.at[m, i], *move_sems(m, first), MOVE_STEPS[i]
                ).start()

    def arrivals(m, first):
        moves(m, first).wait_recv()
        tiles = []
        for k in (4,) if first else (0, 2):
            one, two = got[m, k], got[m, k + 1]
            top = jnp.where(lower, one, turned(two))
            bottom = jnp.where(lower, turned(one), two)
            tiles.append(jnp.concatenate([top, bottom], axis=0))
        return jnp.concatenate(tiles, axis=1)

    def sent(h):
        for kind in range(4):
            halo_kind(h, kind).wait_send()

    plane[0] = jnp.zeros((2, PLANE, 128), F32)
    x_send[...] = jnp.zeros(x_send.shape, F32)
    same_z = jnp.where(iota((PLANE, SIDE), 0) & 7 == iota((PLANE, SIDE), 1), 1.0, 0.0)
    same_y = iota((PLANE, PLANE), 0) >> 3 == iota((PLANE, PLANE), 1) & 7
    goes = (iota((PLANE, SIDE * LANES), 0) >> 3) * LANES + 20
    goes = jnp.where(iota((PLANE, SIDE * LANES), 1) == goes, 1.0, 0.0).astype(BF16)
    rate = jnp.zeros((PLANE, SIDE * LANES), F32)
    for part in parts(load("mix_rate")[...]):
        along_z = jnp.where(same_y, dot_nt(same_z.astype(BF16), part), 0.0)
        rate = rate + dot(along_z.astype(BF16), goes)
    mean_ref = load("mean_field")
    for x in range(SIDE):
        base = LANES * (x % 4)
        plane[0, x // 4, :, base : base + 20] = mean_ref[PLANE * x : PLANE * (x + 1), :]
    field1 = compact((jnp.concatenate([plane[0, 0], plane[0, 1]], axis=1) + rate).T)
    prepare_near(0, field1)

    pl.semaphore_wait(barrier, len(halo_steps))
    send_near(0)

    ok = [
        jnp.where(gx > 0, 1.0, 0.0),
        jnp.where(gx < n_gx - 1, 1.0, 0.0),
        jnp.where(gy > 0, 1.0, 0.0),
        jnp.where(gy < n_gy - 1, 1.0, 0.0),
    ]

    cell1 = load("cell_first")
    off1 = load("offset_first")
    face1 = load("face_first")
    cell2 = load("cell_second")
    cell3 = load("cell_final")
    mass = load("particle_mass")
    off2 = load("offset_second")
    pay[0:20, :] = load("scalars")[...]
    pay[20:21, :] = mass[...]
    pay[21:24, :] = off2[...]
    pay[24:25, :] = cell2[...].astype(F32)
    pay[25:26, :] = cell3[...].astype(F32)
    pay[26:27, :] = cell1[...].astype(F32)
    pay[27:30, :] = off1[...]
    pay[30:32, :] = jnp.zeros((2, pay.shape[1]), F32)

    def packed_movers(faces):
        slots = slots_of(faces)
        hot = [slots_hot(slots[:, lanes]) for lanes in OWN]
        left = [pack_operand(pay[:, lanes]) for lanes in OWN]
        block = sum(dot_nt(a, b) for a, b in zip(left, hot))
        return block[:32] + block[32:]

    def weights_at(cells, offsets, lanes):
        return weights(cells[:, lanes], [offsets[d : d + 1, lanes] for d in range(3)], ok)

    def scalars_of(block):
        row = iota((ROWS, block.shape[1]), 0)
        return jnp.where(row == 20, 1.0, jnp.where(row < 20, block[:ROWS], 0.0))

    def message(values, block):
        row = iota((ROWS, block.shape[1]), 0)
        return jnp.concatenate([jnp.where(row < 20, values, block[:ROWS]), block[ROWS:]], axis=0)

    def work(values, sampled, outer, ws):
        more = gather(outer, ws, 1)
        return react(values, [a + b for a, b in zip(sampled, more)], first, second)

    def work_movers(m, movers, inner, outer, ws):
        blocks = [movers[:, lanes] for lanes in (FAR, NEAR)]
        new = work([scalars_of(block) for block in blocks], inner, outer, ws)
        messages = [message(one, block) for one, block in zip(new, blocks)]
        for first, one in zip((4, 0), messages):
            send_moves(m, first, one)

    movers = packed_movers(face1[...])
    mover_cells = movers[26:27].astype(jnp.int32)
    w_movers = [weights_at(mover_cells, movers[27:30], lanes) for lanes in (FAR, NEAR)]

    rows_buf[...] = jnp.zeros(rows_buf.shape, F32)
    rows_buf[0, 0:20, :] = load("react_in")[...]
    rows_buf[0, 20:21, :] = load("hidden_bias")[...]
    rows_buf[1, 0:20, :] = load("react_out")[...]
    high, low = parts_wide(rows_buf[0])
    first = jnp.concatenate(
        [high, high, low, jnp.zeros((128 - 3 * ROWS, 128), F32)], axis=0
    ).T.astype(BF16)
    high, low = parts_wide(rows_buf[1])
    second = jnp.concatenate(
        [
            jnp.concatenate([high, high], axis=1),
            jnp.concatenate([low, jnp.zeros_like(low)], axis=1),
        ],
        axis=0,
    ).astype(BF16)

    left, outer = send_y(0, field1)
    in_movers = gather(left, w_movers, 0)
    w_own = [weights_at(cell1, off1, lanes) for lanes in OWN]
    in_own = gather(left, w_own, 0)

    outer = outer_left(0, outer)
    work_movers(0, movers, in_movers, outer, w_movers)

    values = work([scalars_of(pay[:, lanes]) for lanes in OWN], in_own, outer, w_own)
    stay = [jnp.where(face1[:, lanes] == 0, mass[:, lanes], 0.0) for lanes in OWN]
    sums = scatter([(v, m, cell2[:, lanes]) for v, m, lanes in zip(values, stay, OWN)])
    for one, lanes in zip(values, OWN):
        pay[0:20, lanes] = one[:20]

    lane = iota((1, 128), 1)
    alive = {
        0: jnp.concatenate([jnp.where(lane < 64, ok[0], ok[1]), jnp.ones((1, 128), F32)], axis=1),
        4: jnp.where(lane < 64, ok[2], ok[3]),
    }

    came = {}
    for i in (0, 4):
        block = arrivals(0, i)
        came[i] = block
        cells = block[24:25].astype(jnp.int32)
        sums = sums + scatter([(scalars_of(block), block[20:21] * alive[i], cells)])
    field2 = average(by_cell(sums), field1)
    prepare_near(1, field2)
    send_near(1)

    face2 = load("face_second")
    movers = packed_movers(face2[...])
    mover_cells = movers[24:25].astype(jnp.int32)
    w_movers = [weights_at(mover_cells, movers[21:24], lanes) for lanes in (FAR, NEAR)]
    left, outer = send_y(1, field2)
    in_movers = gather(left, w_movers, 0)
    w_own = [weights_at(cell2, off2, lanes) for lanes in OWN]
    w_own += [
        weights_at(block[24:25].astype(jnp.int32), block[21:24], slice(None))
        for block in came.values()
    ]
    in_own = gather(left, w_own, 0)

    outer = outer_left(1, outer)
    work_movers(1, movers, in_movers, outer, w_movers)

    values = work(values + [scalars_of(block) for block in came.values()], in_own, outer, w_own)
    masses = [
        jnp.where(face1[:, lanes] + face2[:, lanes] == 0, mass[:, lanes], 0.0) for lanes in OWN
    ] + [block[20:21] * alive[i] for i, block in came.items()]
    cells = [cell3[:, lanes] for lanes in OWN]
    cells += [block[25:26].astype(jnp.int32) for block in came.values()]
    sums = scatter(list(zip(values, masses, cells)))

    sent(0)
    sent(1)
    for i in (0, 4):
        moves(0, i).wait_send()

    for i in (0, 4):
        block = arrivals(1, i)
        cells = block[25:26].astype(jnp.int32)
        sums = sums + scatter([(scalars_of(block), block[20:21] * alive[i], cells)])
    sums = by_cell(sums)
    put(4, spread(average(sums, field2)).T)
    for x in range(SIDE):
        base = LANES * (x % 4)
        out_ref[PLANE * x : PLANE * (x + 1), :] = plane[4, x // 4, :, base : base + 20]

    for i in (0, 4):
        moves(1, i).wait_send()


def shards(
    sizes,
    scalars,
    particle_mass,
    cell_first,
    cell_second,
    cell_final,
    offset_first,
    offset_second,
    face_first,
    face_second,
    mean_field,
    mix_rate,
    react_in,
    hidden_bias,
    react_out,
):
    row = lambda a: a.reshape(1, -1)
    operands = [
        scalars,
        row(particle_mass),
        row(cell_first),
        row(cell_second),
        row(cell_final),
        offset_first,
        offset_second,
        row(face_first),
        row(face_second),
        mean_field.transpose(1, 2, 3, 0).reshape(SIDE * PLANE, 20),
        mix_rate.reshape(PLANE, SIDE),
        react_in.T,
        row(hidden_bias),
        react_out,
    ]
    operands = [pltpu.with_memory_space_constraint(a, pltpu.HBM) for a in operands]
    vmem = pl.BlockSpec(memory_space=pltpu.VMEM)
    result = pl.pallas_call(
        functools.partial(kernel, sizes),
        out_shape=jax.ShapeDtypeStruct((SIDE * PLANE, 20), F32),
        in_specs=[pl.BlockSpec(memory_space=pltpu.HBM)] * len(operands),
        out_specs=vmem,
        scratch_shapes=[pltpu.VMEM(a.shape, a.dtype) for a in operands]
        + [
            pltpu.VMEM((5, 2, PLANE, 128), F32),
            pltpu.VMEM((2, 2, 2, SIDE, 128), F32),
            pltpu.VMEM((2, 2, 4, 1, 128), F32),
            pltpu.VMEM((2, 2, ROWS, 128), F32),
            pltpu.VMEM((2, 8, SIDE, 128), F32),
            pltpu.VMEM((2, 2, 2, SIDE, 128), F32),
            pltpu.VMEM((2, 2, 4, 1, 128), F32),
            pltpu.VMEM((2, 2, ROWS, 128), F32),
            pltpu.VMEM((2, 6, 16, 128), F32),
            pltpu.VMEM((2, 6, 16, 128), F32),
            pltpu.VMEM((2, ROWS, 128), F32),
            pltpu.VMEM((32, 1024), F32),
            pltpu.SemaphoreType.DMA((INPUTS,)),
            pltpu.SemaphoreType.DMA((2, 4)),
            pltpu.SemaphoreType.DMA((2, 4)),
            pltpu.SemaphoreType.DMA((2, 2)),
            pltpu.SemaphoreType.DMA((2, 2)),
        ],
        compiler_params=pltpu.CompilerParams(
            collective_id=0, has_side_effects=True, vmem_limit_bytes=40 * 1024 * 1024
        ),
    )(*operands)
    return result.reshape(SIDE, SIDE, SIDE, 20).transpose(3, 0, 1, 2)


def solution(mesh):
    particles = P(("gx", "gy", "gz"))
    in_specs = (
        P(None, ("gx", "gy", "gz")),
        particles,
        particles,
        particles,
        particles,
        P(None, ("gx", "gy", "gz")),
        P(None, ("gx", "gy", "gz")),
        particles,
        particles,
        P(None, "gx", "gy", "gz"),
        P("gx", "gy", "gz"),
        P(),
        P(),
        P(),
    )
    sizes = (mesh.shape["gx"], mesh.shape["gy"], mesh.shape["gz"])
    return jax.shard_map(
        functools.partial(shards, sizes),
        mesh=mesh,
        in_specs=in_specs,
        out_specs=P(None, "gx", "gy", "gz"),
        check_vma=False,
    )
```

time: 46.4 us -> 46.1 us (level)
  no operation moved by 1% of the time
where the time goes in v2:
time: 46.1 us; the launch traced here: 45.9 us
  Pallas kernels  45.2 us (98%)
  local copies, waits for them, and re-layouts  0.71 us (2%)
    pallas_call x1, Pallas kernels, shards(): pl.pallas_call(functools.partial(kernel, sizes), out_shape=jax.ShapeDtype...  45.2 us

profile of v2, /device:TPU:1, one launch (start us, length us, event | category | flops | bytes accessed | tf_op | source)
XLA Modules:
  0.0 45.9 jit_solution(12059392272780143384)
XLA Ops:
  0.0 45.2 %shard_map.136 = f32[512,20]{1,0:T(8,128)S(1)} custom-call(f32[20,1024]{1,0:T(8,128)} %refs_0_.1, f32[1,1024]{1,0:T(1,128)} %bitcast.19, s32[1,1024]{1,0:T(1,128)} %bitcast.20, s32[1,1024]{1,0:T(1,128)} %bitcast.21, s32[1,1024]{1,0:T(1,128)} %bitcast.22, f32[3,1024]{1,0:T(4,128)} %refs_5_.1, f32[3,1024]{1,0:T(4,128)} %refs_6_.1, s32[1,1024]{1,0:T(1,128)} %bitcast.23, ...), custom_call_target="tpu_custom_call" | custom-call | tf_op jit(solution)/shard_map/pallas_call | solution.py:628
  45.2 0.7 %copy.16 = f32[20,8,8,8]{0,3,2,1:T(8,128)} copy(f32[20,8,8,8]{0,3,2,1:T(8,128)S(1)} %bitcast.15) | data formatting | bytes 81920

commit v3 on v2

--- a/solution.py
+++ b/solution.py
@@ -137,8 +137,17 @@
 
 def left_outer(outer):
     high, low = parts_wide(outer)
-    turned = jnp.concatenate([high, low], axis=0).T[: (SIDE + 2) * ROWS]
-    return jnp.concatenate([turned, turned[:, :PLANE]], axis=1).astype(BF16)
+    turned = jnp.concatenate([high, low], axis=0).T
+    base = SIDE * LANES
+    rows = jnp.concatenate(
+        [
+            compact(turned[:base]),
+            turned[base + 3 * LANES : base + 3 * LANES + ROWS],
+            turned[base : base + ROWS],
+        ],
+        axis=0,
+    )
+    return jnp.concatenate([rows, rows[:, :PLANE]], axis=1).astype(BF16)
 
 
 def gather_own(result, x_in):
@@ -261,7 +270,6 @@
         z_send,
         c_send,
         x_send,
-        near_got,
         tile_got,
         row_got,
         x_got,
@@ -286,20 +294,24 @@
     def at(dx, dy, dz):
         return near_x[dx], near_y[dy], near_z[dz]
 
-    signs = (1, -1)
-    y_steps = [(0, dy, 0) for dy in signs]
-    near_steps = [(dx, 0, dz) for dz in signs for dx in signs]
-    near_steps += [(0, 0, dz) for dz in signs]
-    x_steps = [(dx, 0, 0) for dx in signs]
-    halo_steps = near_steps + x_steps + y_steps
-
-    barrier = pltpu.get_barrier_semaphore()
-    for step in halo_steps:
-        pl.semaphore_signal(barrier, inc=1, device_id=at(*step), device_id_type=MESH)
+    faces = [(1, 0), (-1, 0), (0, 1), (0, -1)]
+    corners = [(1, 1), (1, -1), (-1, 1), (-1, -1)]
+    x_steps = [1, -1]
+    halo_steps = [(dx, dy, dz) for dx in x_steps for dy, dz in corners]
+    halo_steps += [(0, dy, dz) for dy, dz in corners]
+    halo_steps += [(dx, dy, 0) for dx in x_steps for dy in (1, -1)]
+    halo_steps += [(0, dy, 0) for dy in (1, -1)]
+    halo_steps += [(dx, 0, dz) for dx in x_steps for dz in (1, -1)]
+    halo_steps += [(0, 0, dz) for dz in (1, -1)]
+    halo_steps += [(dx, 0, 0) for dx in x_steps]
+
     loads = {
         name: pltpu.make_async_copy(a, to, local_sem.at[i])
         for i, (name, a, to) in enumerate(zip(NAMES, inputs, local))
     }
+    barrier = pltpu.get_barrier_semaphore()
+    for step in halo_steps:
+        pl.semaphore_signal(barrier, inc=1, device_id=at(*step), device_id_type=MESH)
     for name in ORDER:
         loads[name].start()
 
@@ -325,67 +337,87 @@
         return remote_copy(buffer, buffer, send_sem, recv_sem, (1, 0, 0))
 
     def halo_kind(h, kind):
-        buffer = (x_got, near_got, tile_got, row_got)[kind].at[h]
+        buffer = (tile_got, row_got, x_got)[kind].at[h]
         return all_of(buffer, halo_send_sem.at[h, kind], halo_recv_sem.at[h, kind])
 
-    def send_halo(h, kind, steps, source, target):
-        for step, src, dst in zip(steps, source, target):
+    def send_halo(h, first, kind, source, target):
+        for i, (src, dst) in enumerate(zip(source, target)):
             remote_copy(
-                src, dst, halo_send_sem.at[h, kind], halo_recv_sem.at[h, kind], step
+                src, dst, halo_send_sem.at[h, kind], halo_recv_sem.at[h, kind], halo_steps[first + i]
             ).start()
 
-    def prepare_near(h, field):
+    def prepare_x(h, field):
         x_send[h, 0, :, 0:PLANE] = field[7 * ROWS : 8 * ROWS]
         x_send[h, 1, :, 0:PLANE] = field[0:ROWS]
-        put(h, jnp.concatenate([field, jnp.zeros((64, PLANE), F32)], axis=0).T)
+
+    def send_x(h):
+        send_halo(h, 24, 2, [x_send.at[h, k] for k in range(2)], [x_got.at[h, k] for k in range(2)])
+
+    def prepare_corners(h):
+        for slot, row in enumerate((63, 56, 7, 0)):
+            for half in range(2):
+                c_send[h, slot, half] = plane[h, half, row : row + 1, :]
+
+    def prepare_z(h):
         for z, slot in ((7, 0), (0, 1)):
             for half in range(2):
                 z_send[h, slot, half] = plane[h, half, pl.ds(z, SIDE, stride=SIDE), :]
 
-    def send_near(h):
-        source = [z_send.at[h, slot, half] for slot in range(2) for half in (1, 0)]
-        target = [near_got.at[h, 4 + 2 * slot + k] for slot in range(2) for k in range(2)]
+    def send_y(h):
+        sides = ((0, 1), (1, 0))
+        source = [c_send.at[h, slot, half] for _, half in sides for slot in range(4)]
+        target = [row_got.at[h, 8 + 4 * k + slot] for k, _ in sides for slot in range(4)]
+        source += [c_send.at[h, slot] for slot in range(4)]
+        target += [row_got.at[h, 2 * slot : 2 * slot + 2] for slot in range(4)]
+        send_halo(h, 0, 1, source, target)
+        rows = plane.at[h]
+        y_rows = (slice(56, 64), slice(0, 8))
+        source = [rows.at[half, y] for _, half in sides for y in y_rows]
+        target = [tile_got.at[h, 8 + 4 * k + slot] for k, _ in sides for slot in range(2)]
+        source += [rows.at[:, y] for y in y_rows]
+        target += [tile_got.at[h, 2 * slot : 2 * slot + 2] for slot in range(2)]
+        send_halo(h, 12, 0, source, target)
+
+    def send_z(h):
+        sides = ((0, 1), (1, 0))
+        source = [z_send.at[h, slot, half] for _, half in sides for slot in range(2)]
+        target = [tile_got.at[h, 10 + 4 * k + slot] for k, _ in sides for slot in range(2)]
         source += [z_send.at[h, slot] for slot in range(2)]
-        target += [near_got.at[h, 2 * slot : 2 * slot + 2] for slot in range(2)]
-        send_halo(h, 1, near_steps, source, target)
-        send_halo(h, 0, x_steps, [x_send.at[h, k] for k in range(2)], [x_got.at[h, k] for k in range(2)])
-
-    def send_y(h, field):
-        halo_kind(h, 0).wait_recv()
+        target += [tile_got.at[h, 4 + 2 * slot : 6 + 2 * slot] for slot in range(2)]
+        send_halo(h, 18, 0, source, target)
+
+    def stack_outer(face, corner):
+        row = iota((SIDE, 128), 0)
+        last = jnp.zeros((SIDE, 128), F32)
+        for slot in range(4):
+            last = jnp.where(row == slot, corner[slot], last)
+        none = jnp.zeros((PLANE - 5 * SIDE, 128), F32)
+        return jnp.concatenate(face + [last, none], axis=0)
+
+    def inner_left(h, field):
+        halo_kind(h, 2).wait_recv()
         sides = jnp.concatenate([x_got[h, 0], x_got[h, 1]], axis=0)[:, :PLANE]
-        put(h + 2, jnp.concatenate([field, sides, jnp.zeros((16, PLANE), F32)], axis=0).T)
-        rows = plane.at[h + 2]
-        y_rows = (slice(56, 64), slice(0, 8))
-        send_halo(h, 2, y_steps, [rows.at[:, y] for y in y_rows], [tile_got.at[h, k] for k in range(2)])
-        halo_kind(h, 1).wait_recv()
-        lane = iota((SIDE, 128), 1)
-        outer = []
-        for slot in range(2):
-            low = pltpu.roll(near_got[h, 4 + 2 * slot], 24, 1)
-            high = pltpu.roll(near_got[h, 5 + 2 * slot], 88, 1)
-            second_half = jnp.where(
-                lane < 64, near_got[h, 2 * slot + 1], jnp.where(lane < 88, low, high)
+        return jnp.concatenate([left_of(field), left_of(sides)], axis=0)
+
+    def outer_left(h):
+        for kind in range(2):
+            halo_kind(h, kind).wait_recv()
+        both = [
+            stack_outer(
+                [tile_got[h, 2 * slot + half] for slot in range(4)],
+                [row_got[h, 2 * slot + half] for slot in range(4)],
             )
-            halves = (near_got[h, 2 * slot], second_half)
-            outer.append(jnp.concatenate(halves, axis=1))
-            for half in range(2):
-                c_send[h, 0, 2 * slot + half] = halves[half][7:8]
-                c_send[h, 1, 2 * slot + half] = halves[half][0:1]
-        send_halo(h, 3, y_steps, [c_send.at[h, k] for k in range(2)], [row_got.at[h, k] for k in range(2)])
-        return jnp.concatenate([left_of(field), left_of(sides)], axis=0), outer
-
-    def outer_left(h, outer):
-        for kind in (2, 3):
-            halo_kind(h, kind).wait_recv()
-        faces = [jnp.concatenate([tile_got[h, k, 0], tile_got[h, k, 1]], axis=1) for k in range(2)]
-        row = iota((SIDE, 256), 0)
-        last = jnp.zeros((SIDE, 256), F32)
-        for k in range(2):
-            for slot in range(2):
-                one = [row_got[h, k, 2 * slot + half] for half in range(2)]
-                last = jnp.where(row == 2 * k + slot, jnp.concatenate(one, axis=1), last)
-        none = jnp.zeros((PLANE - 5 * SIDE, 256), F32)
-        return left_outer(jnp.concatenate(faces + outer + [last, none], axis=0))
+            for half in range(2)
+        ]
+        side = [
+            stack_outer(
+                [tile_got[h, 8 + 4 * k + slot] for slot in range(4)],
+                [row_got[h, 8 + 4 * k + slot] for slot in range(4)],
+            )
+            for k in range(2)
+        ]
+        last = jnp.where(iota((PLANE, 128), 1) < PLANE, side[1], side[0])
+        return left_outer(jnp.concatenate(both + [last], axis=1))
 
     lower = iota((16, 128), 1) < BLOCK
 
@@ -420,7 +452,7 @@
         return jnp.concatenate(tiles, axis=1)
 
     def sent(h):
-        for kind in range(4):
+        for kind in range(3):
             halo_kind(h, kind).wait_send()
 
     plane[0] = jnp.zeros((2, PLANE, 128), F32)
@@ -437,11 +469,17 @@
     for x in range(SIDE):
         base = LANES * (x % 4)
         plane[0, x // 4, :, base : base + 20] = mean_ref[PLANE * x : PLANE * (x + 1), :]
-    field1 = compact((jnp.concatenate([plane[0, 0], plane[0, 1]], axis=1) + rate).T)
-    prepare_near(0, field1)
+    inner1 = jnp.concatenate([plane[0, 0], plane[0, 1]], axis=1) + rate
+    put(0, inner1)
+    prepare_corners(0)
+    prepare_z(0)
+    field1 = compact(inner1.T)
+    prepare_x(0, field1)
 
     pl.semaphore_wait(barrier, len(halo_steps))
-    send_near(0)
+    send_y(0)
+    send_z(0)
+    send_x(0)
 
     ok = [
         jnp.where(gx > 0, 1.0, 0.0),
@@ -516,12 +554,12 @@
         axis=0,
     ).astype(BF16)
 
-    left, outer = send_y(0, field1)
+    left = inner_left(0, field1)
     in_movers = gather(left, w_movers, 0)
     w_own = [weights_at(cell1, off1, lanes) for lanes in OWN]
     in_own = gather(left, w_own, 0)
 
-    outer = outer_left(0, outer)
+    outer = outer_left(0)
     work_movers(0, movers, in_movers, outer, w_movers)
 
     values = work([scalars_of(pay[:, lanes]) for lanes in OWN], in_own, outer, w_own)
@@ -543,14 +581,19 @@
         cells = block[24:25].astype(jnp.int32)
         sums = sums + scatter([(scalars_of(block), block[20:21] * alive[i], cells)])
     field2 = average(by_cell(sums), field1)
-    prepare_near(1, field2)
-    send_near(1)
+    put(1, spread(field2).T)
+    prepare_corners(1)
+    send_y(1)
+    prepare_z(1)
+    send_z(1)
+    prepare_x(1, field2)
+    send_x(1)
 
     face2 = load("face_second")
     movers = packed_movers(face2[...])
     mover_cells = movers[24:25].astype(jnp.int32)
     w_movers = [weights_at(mover_cells, movers[21:24], lanes) for lanes in (FAR, NEAR)]
-    left, outer = send_y(1, field2)
+    left = inner_left(1, field2)
     in_movers = gather(left, w_movers, 0)
     w_own = [weights_at(cell2, off2, lanes) for lanes in OWN]
     w_own += [
@@ -559,7 +602,7 @@
     ]
     in_own = gather(left, w_own, 0)
 
-    outer = outer_left(1, outer)
+    outer = outer_left(1)
     work_movers(1, movers, in_movers, outer, w_movers)
 
     values = work(values + [scalars_of(block) for block in came.values()], in_own, outer, w_own)
@@ -580,10 +623,9 @@
         cells = block[25:26].astype(jnp.int32)
         sums = sums + scatter([(scalars_of(block), block[20:21] * alive[i], cells)])
     sums = by_cell(sums)
-    put(4, spread(average(sums, field2)).T)
+    result = spread(average(sums, field2)).T
     for x in range(SIDE):
-        base = LANES * (x % 4)
-        out_ref[PLANE * x : PLANE * (x + 1), :] = plane[4, x // 4, :, base : base + 20]
+        out_ref[PLANE * x : PLANE * (x + 1), :] = result[:, LANES * x : LANES * x + 20]
 
     for i in (0, 4):
         moves(1, i).wait_send()
@@ -632,21 +674,20 @@
         out_specs=vmem,
         scratch_shapes=[pltpu.VMEM(a.shape, a.dtype) for a in operands]
         + [
-            pltpu.VMEM((5, 2, PLANE, 128), F32),
+            pltpu.VMEM((2, 2, PLANE, 128), F32),
             pltpu.VMEM((2, 2, 2, SIDE, 128), F32),
-            pltpu.VMEM((2, 2, 4, 1, 128), F32),
+            pltpu.VMEM((2, 4, 2, 1, 128), F32),
             pltpu.VMEM((2, 2, ROWS, 128), F32),
-            pltpu.VMEM((2, 8, SIDE, 128), F32),
-            pltpu.VMEM((2, 2, 2, SIDE, 128), F32),
-            pltpu.VMEM((2, 2, 4, 1, 128), F32),
+            pltpu.VMEM((2, 16, SIDE, 128), F32),
+            pltpu.VMEM((2, 16, 1, 128), F32),
             pltpu.VMEM((2, 2, ROWS, 128), F32),
             pltpu.VMEM((2, 6, 16, 128), F32),
             pltpu.VMEM((2, 6, 16, 128), F32),
             pltpu.VMEM((2, ROWS, 128), F32),
             pltpu.VMEM((32, 1024), F32),
             pltpu.SemaphoreType.DMA((INPUTS,)),
-            pltpu.SemaphoreType.DMA((2, 4)),
-            pltpu.SemaphoreType.DMA((2, 4)),
+            pltpu.SemaphoreType.DMA((2, 3)),
+            pltpu.SemaphoreType.DMA((2, 3)),
             pltpu.SemaphoreType.DMA((2, 2)),
             pltpu.SemaphoreType.DMA((2, 2)),
         ],

time: 46.1 us -> 44.1 us (0.957)
  Pallas kernels: 45.2 us -> 43.2 us
    pallas_call x1, Pallas kernels: 45.2 us -> 43.2 us  [shards(): pl.pallas_call(functools.partial(kernel, sizes), out_shape=jax.ShapeDtype...]
where the time goes in v3:
time: 44.1 us; the launch traced here: 44 us
  Pallas kernels  43.2 us (98%)
  local copies, waits for them, and re-layouts  0.71 us (2%)
    pallas_call x1, Pallas kernels, shards(): pl.pallas_call(functools.partial(kernel, sizes), out_shape=jax.ShapeDtype...  43.2 us

profile of v3, /device:TPU:1, one launch (start us, length us, event | category | flops | bytes accessed | tf_op | source)
XLA Modules:
  0.0 44.0 jit_solution(5690262071847451694)
XLA Ops:
  0.0 43.2 %shard_map.136 = f32[512,20]{1,0:T(8,128)S(1)} custom-call(f32[20,1024]{1,0:T(8,128)} %refs_0_.1, f32[1,1024]{1,0:T(1,128)} %bitcast.19, s32[1,1024]{1,0:T(1,128)} %bitcast.20, s32[1,1024]{1,0:T(1,128)} %bitcast.21, s32[1,1024]{1,0:T(1,128)} %bitcast.22, f32[3,1024]{1,0:T(4,128)} %refs_5_.1, f32[3,1024]{1,0:T(4,128)} %refs_6_.1, s32[1,1024]{1,0:T(1,128)} %bitcast.23, ...), custom_call_target="tpu_custom_call" | custom-call | tf_op jit(solution)/shard_map/pallas_call | solution.py:670
  43.3 0.7 %copy.16 = f32[20,8,8,8]{0,3,2,1:T(8,128)} copy(f32[20,8,8,8]{0,3,2,1:T(8,128)S(1)} %bitcast.15) | data formatting | bytes 81920

commit v4 on v3

--- a/solution.py
+++ b/solution.py
@@ -478,8 +478,8 @@
 
     pl.semaphore_wait(barrier, len(halo_steps))
     send_y(0)
+    send_x(0)
     send_z(0)
-    send_x(0)
 
     ok = [
         jnp.where(gx > 0, 1.0, 0.0),
@@ -554,9 +554,9 @@
         axis=0,
     ).astype(BF16)
 
+    w_own = [weights_at(cell1, off1, lanes) for lanes in OWN]
     left = inner_left(0, field1)
     in_movers = gather(left, w_movers, 0)
-    w_own = [weights_at(cell1, off1, lanes) for lanes in OWN]
     in_own = gather(left, w_own, 0)
 
     outer = outer_left(0)
@@ -584,22 +584,22 @@
     put(1, spread(field2).T)
     prepare_corners(1)
     send_y(1)
+    prepare_x(1, field2)
+    send_x(1)
     prepare_z(1)
     send_z(1)
-    prepare_x(1, field2)
-    send_x(1)
 
     face2 = load("face_second")
     movers = packed_movers(face2[...])
     mover_cells = movers[24:25].astype(jnp.int32)
     w_movers = [weights_at(mover_cells, movers[21:24], lanes) for lanes in (FAR, NEAR)]
-    left = inner_left(1, field2)
-    in_movers = gather(left, w_movers, 0)
     w_own = [weights_at(cell2, off2, lanes) for lanes in OWN]
     w_own += [
         weights_at(block[24:25].astype(jnp.int32), block[21:24], slice(None))
         for block in came.values()
     ]
+    left = inner_left(1, field2)
+    in_movers = gather(left, w_movers, 0)
     in_own = gather(left, w_own, 0)
 
     outer = outer_left(1)

time: 44.1 us -> 44.1 us (level)
  no operation moved by 1% of the time
where the time goes in v4:
time: 44.1 us; the launch traced here: 44 us
  Pallas kernels  43.2 us (98%)
  local copies, waits for them, and re-layouts  0.71 us (2%)
    pallas_call x1, Pallas kernels, shards(): pl.pallas_call(functools.partial(kernel, sizes), out_shape=jax.ShapeDtype...  43.2 us

profile of v4, /device:TPU:1, one launch (start us, length us, event | category | flops | bytes accessed | tf_op | source)
XLA Modules:
  0.0 44.0 jit_solution(10676189198040896362)
XLA Ops:
  0.0 43.2 %shard_map.136 = f32[512,20]{1,0:T(8,128)S(1)} custom-call(f32[20,1024]{1,0:T(8,128)} %refs_0_.1, f32[1,1024]{1,0:T(1,128)} %bitcast.19, s32[1,1024]{1,0:T(1,128)} %bitcast.20, s32[1,1024]{1,0:T(1,128)} %bitcast.21, s32[1,1024]{1,0:T(1,128)} %bitcast.22, f32[3,1024]{1,0:T(4,128)} %refs_5_.1, f32[3,1024]{1,0:T(4,128)} %refs_6_.1, s32[1,1024]{1,0:T(1,128)} %bitcast.23, ...), custom_call_target="tpu_custom_call" | custom-call | tf_op jit(solution)/shard_map/pallas_call | solution.py:670
  43.2 0.7 %copy.16 = f32[20,8,8,8]{0,3,2,1:T(8,128)} copy(f32[20,8,8,8]{0,3,2,1:T(8,128)S(1)} %bitcast.15) | data formatting | bytes 81920

commit v5 on v4

--- a/solution.py
+++ b/solution.py
@@ -527,11 +527,10 @@
         return react(values, [a + b for a, b in zip(sampled, more)], first, second)
 
     def work_movers(m, movers, inner, outer, ws):
-        blocks = [movers[:, lanes] for lanes in (FAR, NEAR)]
-        new = work([scalars_of(block) for block in blocks], inner, outer, ws)
-        messages = [message(one, block) for one, block in zip(new, blocks)]
-        for first, one in zip((4, 0), messages):
-            send_moves(m, first, one)
+        for i, (first, lanes) in enumerate(((4, FAR), (0, NEAR))):
+            block = movers[:, lanes]
+            new = work([scalars_of(block)], inner[i : i + 1], outer, ws[i : i + 1])
+            send_moves(m, first, message(new[0], block))
 
     movers = packed_movers(face1[...])
     mover_cells = movers[26:27].astype(jnp.int32)

time: 44.1 us -> 44.3 us (level)
  no operation moved by 1% of the time
where the time goes in v5:
time: 44.3 us; the launch traced here: 44.2 us
  Pallas kernels  43.5 us (98%)
  local copies, waits for them, and re-layouts  0.71 us (2%)
    pallas_call x1, Pallas kernels, shards(): pl.pallas_call(functools.partial(kernel, sizes), out_shape=jax.ShapeDtype...  43.5 us

profile of v5, /device:TPU:1, one launch (start us, length us, event | category | flops | bytes accessed | tf_op | source)
XLA Modules:
  0.0 44.2 jit_solution(17732144545863314392)
XLA Ops:
  0.0 43.5 %shard_map.136 = f32[512,20]{1,0:T(8,128)S(1)} custom-call(f32[20,1024]{1,0:T(8,128)} %refs_0_.1, f32[1,1024]{1,0:T(1,128)} %bitcast.19, s32[1,1024]{1,0:T(1,128)} %bitcast.20, s32[1,1024]{1,0:T(1,128)} %bitcast.21, s32[1,1024]{1,0:T(1,128)} %bitcast.22, f32[3,1024]{1,0:T(4,128)} %refs_5_.1, f32[3,1024]{1,0:T(4,128)} %refs_6_.1, s32[1,1024]{1,0:T(1,128)} %bitcast.23, ...), custom_call_target="tpu_custom_call" | custom-call | tf_op jit(solution)/shard_map/pallas_call | solution.py:669
  43.5 0.7 %copy.16 = f32[20,8,8,8]{0,3,2,1:T(8,128)} copy(f32[20,8,8,8]{0,3,2,1:T(8,128)S(1)} %bitcast.15) | data formatting | bytes 81920
